TPU v7x, 32 devices: a whole 2x2x4 slice. The times are simulated.
32 devices in a mesh: ctx: 8 (over y, x, core), fsdp: 4 (over z).
Axes of the slice: x: 2, y: 2, z: 4, core: 2. Of those that a mesh axis runs over, the one named last changes fastest.
Arguments:
- tokens: bfloat16 [16, 1024, 576], P('fsdp', 'ctx'), may hold values from -6 to 6
- block_order: int32 [16], replicated, may hold values from 0 to 15, each once
- gain_one: bfloat16 [576], P('fsdp'), may hold values from 0.5 to 1.5
- gain_two: bfloat16 [576], P('fsdp'), may hold values from 0.5 to 1.5
- query_weight: bfloat16 [576, 576], P('fsdp'), may hold values from -0.5 to 0.5
- key_matrix: bfloat16 [576, 192], P('fsdp'), may hold values from -0.25 to 0.25
- value_matrix: bfloat16 [576, 192], P('fsdp'), may hold values from -0.25 to 0.25
- out_weight: bfloat16 [576, 576], P('fsdp'), may hold values from -1.5 to 1.5
- gate_weight: bfloat16 [576, 1536], P('fsdp'), may hold values from -0.25 to 0.25
- up_weight: bfloat16 [576, 1536], P('fsdp'), may hold values from -0.25 to 0.25
- down_weight: bfloat16 [1536, 576], P('fsdp'), may hold values from -0.3125 to 0.3125
- cotangent: bfloat16 [16, 1024, 576], P('fsdp', 'ctx'), may hold values from -6 to 6
Outputs:
- output: bfloat16 [16, 1024, 576], P('fsdp', 'ctx')
- grad_tokens: bfloat16 [16, 1024, 576], P('fsdp', 'ctx')
- gain_one_grad: float32 [576], P('fsdp')
- gain_two_grad: float32 [576], P('fsdp')
- query_weight_grad: float32 [576, 576], P('fsdp')
- key_weight_grad: float32 [576, 192], P('fsdp')
- value_weight_grad: float32 [576, 192], P('fsdp')
- out_weight_grad: float32 [576, 576], P('fsdp')
- gate_weight_grad: float32 [576, 1536], P('fsdp')
- up_weight_grad: float32 [576, 1536], P('fsdp')
- down_weight_grad: float32 [1536, 576], P('fsdp')
Inputs may be any that keep to these rules, and one draw needn't show every extreme that they name: A permutation; stored half-block j of every sequence (rows j * 64 to (j + 1) * 64 - 1) holds the tokens of positions block_order[j] * 64 onward.
All inputs are finite; a program needn't handle non-finite values.
Results may differ from a plain program's by a relative error of at most 0.02.
Values may be sent and summed in bfloat16 or wider, within the bound.
A program may use at most 256 MiB of HBM per device.

v0:
```python
import math

import jax
import jax.numpy as jnp
from jax import lax
from jax.sharding import PartitionSpec as P

QUERY_HEADS = 9
KEY_VALUE_HEADS = 3
HEAD_DIMENSION = 64


eps = 1e-05
rope_base = 100000.0
mask_fill_value = -1e30


def row_positions(row_ids, block_order, half_size):
    slot_ids = jnp.arange(block_order.shape[0], dtype=jnp.int32)
    chosen = jnp.sum(
        jnp.where((row_ids // half_size)[:, None] == slot_ids[None, :], block_order[None, :], 0),
        axis=1,
    )
    return chosen * half_size + row_ids % half_size


def rope_tables(token_positions):
    inverse = jnp.exp(
        jnp.arange(HEAD_DIMENSION // 2, dtype=jnp.float32)
        * (-2.0 * math.log(rope_base) / HEAD_DIMENSION)
    )
    angles = token_positions.astype(jnp.float32)[:, None] * inverse[None, :]
    return (jnp.cos(angles), jnp.sin(angles))


def apply_rotary(vectors, cosine_table, sine_table):
    front = vectors[..., : HEAD_DIMENSION // 2]
    back_half = vectors[..., HEAD_DIMENSION // 2 :]
    cos_rows = cosine_table[:, None, :]
    sin_rows = sine_table[:, None, :]
    return jnp.concatenate(
        [front * cos_rows - back_half * sin_rows, back_half * cos_rows + front * sin_rows], axis=-1
    )


def rms_scale(values_in):
    return lax.rsqrt(jnp.mean(values_in * values_in, axis=-1, keepdims=True) + eps)


def norm_back(grad_normed, base_rows, gain_rows, scale_rows):
    scaled = grad_normed * gain_rows
    return scale_rows * (scaled - base_rows * jnp.mean(scaled * base_rows, axis=-1, keepdims=True))


def blockwise(step_fn, carried, arrived, rows_per_block):
    count_rows = arrived[0].shape[1]
    count_of_blocks = count_rows // rows_per_block
    stacked = tuple(
        (
            jnp.moveaxis(
                member.reshape(
                    (member.shape[0], count_of_blocks, rows_per_block) + member.shape[2:]
                ),
                1,
                0,
            )
            for member in arrived
        )
    )
    offsets = jnp.arange(count_of_blocks, dtype=jnp.int32) * rows_per_block

    def scan_step(inner, scan_item):
        return (step_fn(inner, scan_item[1], scan_item[0]), None)

    result, unused = lax.scan(scan_step, carried, (offsets, stacked))
    return result


def body(
    tokens,
    block_order,
    gain_one,
    gain_two,
    query_weight,
    key_matrix,
    value_matrix,
    out_weight,
    gate_weight,
    up_weight,
    down_weight,
    cotangent,
):
    count_of_sequences, rows_per_block, model_width = tokens.shape
    half_size = rows_per_block // 2
    query_group_width = QUERY_HEADS // KEY_VALUE_HEADS
    score_scale = HEAD_DIMENSION ** (-0.5)
    ctx_index = lax.axis_index("ctx")
    gathered = (
        lax.all_gather(gain_one, "fsdp", axis=0, tiled=True),
        lax.all_gather(gain_two, "fsdp", axis=0, tiled=True),
        lax.all_gather(query_weight, "fsdp", axis=0, tiled=True),
        lax.all_gather(key_matrix, "fsdp", axis=0, tiled=True),
        lax.all_gather(value_matrix, "fsdp", axis=0, tiled=True),
        lax.all_gather(out_weight, "fsdp", axis=0, tiled=True),
        lax.all_gather(gate_weight, "fsdp", axis=0, tiled=True),
        lax.all_gather(up_weight, "fsdp", axis=0, tiled=True),
        lax.all_gather(down_weight, "fsdp", axis=0, tiled=True),
    )
    gain_first = gathered[0].astype(jnp.float32)
    gain_second = gathered[1].astype(jnp.float32)
    query_full, key_full, value_full, out_full, gate_full, up_full, down_full = gathered[2:]
    own_positions = row_positions(
        ctx_index * rows_per_block + jnp.arange(rows_per_block, dtype=jnp.int32),
        block_order,
        half_size,
    )
    cosine_table, sine_table = rope_tables(own_positions)
    inputs = tokens.astype(jnp.float32)
    scale_one = rms_scale(inputs)
    base_one = inputs * scale_one
    normed = (base_one * gain_first).astype(jnp.bfloat16)
    query_rows_all = jnp.dot(normed, query_full, preferred_element_type=jnp.float32).reshape(
        count_of_sequences, rows_per_block, QUERY_HEADS, HEAD_DIMENSION
    )
    projected_key = jnp.dot(normed, key_full, preferred_element_type=jnp.float32).reshape(
        count_of_sequences, rows_per_block, KEY_VALUE_HEADS, HEAD_DIMENSION
    )
    projected_value = (
        jnp.dot(normed, value_full, preferred_element_type=jnp.float32)
        .astype(jnp.bfloat16)
        .reshape(count_of_sequences, rows_per_block, KEY_VALUE_HEADS, HEAD_DIMENSION)
    )
    rotary_query = (
        apply_rotary(query_rows_all, cosine_table, sine_table)
        .astype(jnp.bfloat16)
        .reshape(
            count_of_sequences, rows_per_block, KEY_VALUE_HEADS, query_group_width, HEAD_DIMENSION
        )
    )
    rotary_key = apply_rotary(projected_key, cosine_table, sine_table).astype(jnp.bfloat16)

    def far_rows(first_row, count_rows):
        return row_positions(
            first_row + jnp.arange(count_rows, dtype=jnp.int32), block_order, half_size
        )

    def keep_state(kept_state):
        return kept_state

    def forward_block(carried, arrived, first_row):
        far_keys, far_values = arrived
        allowed = own_positions[:, None] >= far_rows(first_row, far_keys.shape[1])[None, :]

        def forward_compute(current):
            scores = (
                jnp.einsum(
                    "sbhgd,snhd->shgbn", rotary_query, far_keys, preferred_element_type=jnp.float32
                )
                * score_scale
            )
            masked = jnp.where(allowed, scores, mask_fill_value)
            new_top = jnp.maximum(current[0], jnp.max(masked, axis=-1))
            exponent = jnp.where(allowed, jnp.exp(masked - new_top[..., None]), 0.0)
            factor = jnp.exp(current[0] - new_top)
            new_total = current[1] * factor + jnp.sum(exponent, axis=-1)
            new_accum = current[2] * factor[..., None] + jnp.einsum(
                "shgbn,snhd->shgbd",
                exponent.astype(jnp.bfloat16),
                far_values,
                preferred_element_type=jnp.float32,
            )
            return (new_top, new_total, new_accum)

        return lax.cond(jnp.any(allowed), forward_compute, keep_state, carried)

    start_state = (
        jnp.full(
            (count_of_sequences, KEY_VALUE_HEADS, query_group_width, rows_per_block),
            mask_fill_value,
            jnp.float32,
        ),
        jnp.zeros(
            (count_of_sequences, KEY_VALUE_HEADS, query_group_width, rows_per_block), jnp.float32
        ),
        jnp.zeros(
            (
                count_of_sequences,
                KEY_VALUE_HEADS,
                query_group_width,
                rows_per_block,
                HEAD_DIMENSION,
            ),
            jnp.float32,
        ),
    )
    row_top, row_total, accum = blockwise(
        forward_block,
        start_state,
        (
            lax.all_gather(rotary_key, "ctx", axis=1, tiled=True),
            lax.all_gather(projected_value, "ctx", axis=1, tiled=True),
        ),
        rows_per_block,
    )
    log_total = row_top + jnp.log(row_total)
    attended_rows = jnp.transpose(accum / row_total[..., None], (0, 3, 1, 2, 4))
    mixed_heads = attended_rows.reshape(
        count_of_sequences, rows_per_block, QUERY_HEADS * HEAD_DIMENSION
    ).astype(jnp.bfloat16)
    middle = inputs + jnp.dot(mixed_heads, out_full, preferred_element_type=jnp.float32)
    scale_two = rms_scale(middle)
    base_two = middle * scale_two
    normed_two = (base_two * gain_second).astype(jnp.bfloat16)
    gate_proj = jnp.dot(normed_two, gate_full, preferred_element_type=jnp.float32)
    up_proj = jnp.dot(normed_two, up_full, preferred_element_type=jnp.float32)
    sigmoid_gate = jax.nn.sigmoid(gate_proj)
    activated = gate_proj * sigmoid_gate
    hidden = (activated * up_proj).astype(jnp.bfloat16)
    output = (middle + jnp.dot(hidden, down_full, preferred_element_type=jnp.float32)).astype(
        jnp.bfloat16
    )
    down_grad = jnp.einsum("sbf,sbd->fd", hidden, cotangent, preferred_element_type=jnp.float32)
    grad_hidden = jnp.einsum(
        "sbd,fd->sbf", cotangent, down_full, preferred_element_type=jnp.float32
    )
    grad_gate = (
        grad_hidden * up_proj * sigmoid_gate * (1.0 + gate_proj * (1.0 - sigmoid_gate))
    ).astype(jnp.bfloat16)
    grad_up = (grad_hidden * activated).astype(jnp.bfloat16)
    gate_grad = jnp.einsum("sbd,sbf->df", normed_two, grad_gate, preferred_element_type=jnp.float32)
    up_grad = jnp.einsum("sbd,sbf->df", normed_two, grad_up, preferred_element_type=jnp.float32)
    grad_normed_two = jnp.einsum(
        "sbf,df->sbd", grad_gate, gate_full, preferred_element_type=jnp.float32
    ) + jnp.einsum("sbf,df->sbd", grad_up, up_full, preferred_element_type=jnp.float32)
    gain_two_grad = jnp.sum(grad_normed_two * base_two, axis=(0, 1))
    grad_middle = cotangent.astype(jnp.float32) + norm_back(
        grad_normed_two, base_two, gain_second, scale_two
    )
    grad_branch = grad_middle.astype(jnp.bfloat16)
    out_grad = jnp.einsum(
        "sbq,sbd->qd", mixed_heads, grad_branch, preferred_element_type=jnp.float32
    )
    mixed_gradient = jnp.einsum(
        "sbd,qd->sbq", grad_branch, out_full, preferred_element_type=jnp.float32
    ).astype(jnp.bfloat16)
    heads_gradient = mixed_gradient.reshape(
        count_of_sequences, rows_per_block, KEY_VALUE_HEADS, query_group_width, HEAD_DIMENSION
    )
    row_delta = jnp.sum(heads_gradient.astype(jnp.float32) * attended_rows, axis=-1)
    delta_here = jnp.transpose(row_delta, (0, 2, 3, 1))
    log_rows = jnp.transpose(log_total, (0, 3, 1, 2))

    def query_block(carried, arrived, first_row):
        far_keys, far_values = arrived
        allowed = own_positions[:, None] >= far_rows(first_row, far_keys.shape[1])[None, :]

        def query_compute(current):
            scores = (
                jnp.einsum(
                    "sbhgd,snhd->shgbn", rotary_query, far_keys, preferred_element_type=jnp.float32
                )
                * score_scale
            )
            probability = jnp.where(
                allowed,
                jnp.exp(jnp.where(allowed, scores - log_total[..., None], mask_fill_value)),
                0.0,
            )
            grad_prob = jnp.einsum(
                "sbhgd,snhd->shgbn", heads_gradient, far_values, preferred_element_type=jnp.float32
            )
            grad_score = (probability * (grad_prob - delta_here[..., None])).astype(jnp.bfloat16)
            return (
                current
                + jnp.einsum(
                    "shgbn,snhd->sbhgd", grad_score, far_keys, preferred_element_type=jnp.float32
                )
                * score_scale
            )

        return lax.cond(jnp.any(allowed), query_compute, keep_state, carried)

    query_sum = blockwise(
        query_block,
        jnp.zeros(
            (
                count_of_sequences,
                rows_per_block,
                KEY_VALUE_HEADS,
                query_group_width,
                HEAD_DIMENSION,
            ),
            jnp.float32,
        ),
        (
            lax.all_gather(rotary_key, "ctx", axis=1, tiled=True),
            lax.all_gather(projected_value, "ctx", axis=1, tiled=True),
        ),
        rows_per_block,
    )
    grad_query = (
        apply_rotary(
            query_sum.reshape(count_of_sequences, rows_per_block, QUERY_HEADS, HEAD_DIMENSION),
            cosine_table,
            -sine_table,
        )
        .astype(jnp.bfloat16)
        .reshape(count_of_sequences, rows_per_block, QUERY_HEADS * HEAD_DIMENSION)
    )

    def key_block(carried, arrived, first_row):
        far_queries, far_grads, far_log, far_delta = arrived
        allowed = far_rows(first_row, far_queries.shape[1])[:, None] >= own_positions[None, :]

        def key_compute(current):
            scores = (
                jnp.einsum(
                    "snhgd,sbhd->shgnb", far_queries, rotary_key, preferred_element_type=jnp.float32
                )
                * score_scale
            )
            log_part = jnp.transpose(far_log, (0, 2, 3, 1))[..., None]
            delta_part = jnp.transpose(far_delta, (0, 2, 3, 1))[..., None]
            probability = jnp.where(
                allowed, jnp.exp(jnp.where(allowed, scores - log_part, mask_fill_value)), 0.0
            )
            grad_prob = jnp.einsum(
                "snhgd,sbhd->shgnb", far_grads, projected_value, preferred_element_type=jnp.float32
            )
            grad_score = (probability * (grad_prob - delta_part)).astype(jnp.bfloat16)
            key_part = (
                current[0]
                + jnp.einsum(
                    "shgnb,snhgd->sbhd", grad_score, far_queries, preferred_element_type=jnp.float32
                )
                * score_scale
            )
            value_part = current[1] + jnp.einsum(
                "shgnb,snhgd->sbhd",
                probability.astype(jnp.bfloat16),
                far_grads,
                preferred_element_type=jnp.float32,
            )
            return (key_part, value_part)

        return lax.cond(jnp.any(allowed), key_compute, keep_state, carried)

    key_start = (
        jnp.zeros(
            (count_of_sequences, rows_per_block, KEY_VALUE_HEADS, HEAD_DIMENSION), jnp.float32
        ),
        jnp.zeros(
            (count_of_sequences, rows_per_block, KEY_VALUE_HEADS, HEAD_DIMENSION), jnp.float32
        ),
    )
    all_stats = (
        lax.all_gather(log_rows, "ctx", axis=1, tiled=True),
        lax.all_gather(row_delta, "ctx", axis=1, tiled=True),
    )

    def stats_block(carried, arrived, first_row):
        count_rows = arrived[0].shape[1]
        log_slice = lax.dynamic_slice_in_dim(all_stats[0], first_row, count_rows, 1)
        delta_slice = lax.dynamic_slice_in_dim(all_stats[1], first_row, count_rows, 1)
        return key_block(carried, (arrived[0], arrived[1], log_slice, delta_slice), first_row)

    key_sum, weighted_value_sum = blockwise(
        stats_block,
        key_start,
        (
            lax.all_gather(rotary_query, "ctx", axis=1, tiled=True),
            lax.all_gather(heads_gradient, "ctx", axis=1, tiled=True),
        ),
        rows_per_block,
    )
    grad_key = (
        apply_rotary(key_sum, cosine_table, -sine_table)
        .astype(jnp.bfloat16)
        .reshape(count_of_sequences, rows_per_block, KEY_VALUE_HEADS * HEAD_DIMENSION)
    )
    value_gradient = weighted_value_sum.astype(jnp.bfloat16).reshape(
        count_of_sequences, rows_per_block, KEY_VALUE_HEADS * HEAD_DIMENSION
    )
    query_grad = jnp.einsum("sbd,sbq->dq", normed, grad_query, preferred_element_type=jnp.float32)
    key_grad = jnp.einsum("sbd,sbq->dq", normed, grad_key, preferred_element_type=jnp.float32)
    value_grad = jnp.einsum(
        "sbd,sbq->dq", normed, value_gradient, preferred_element_type=jnp.float32
    )
    grad_normed = jnp.einsum(
        "sbq,dq->sbd", grad_query, query_full, preferred_element_type=jnp.float32
    )
    grad_normed = grad_normed + jnp.einsum(
        "sbq,dq->sbd", grad_key, key_full, preferred_element_type=jnp.float32
    )
    grad_normed = grad_normed + jnp.einsum(
        "sbq,dq->sbd", value_gradient, value_full, preferred_element_type=jnp.float32
    )
    gain_one_grad = jnp.sum(grad_normed * base_one, axis=(0, 1))
    grad_tokens = (grad_middle + norm_back(grad_normed, base_one, gain_first, scale_one)).astype(
        jnp.bfloat16
    )
    owned = lax.psum(
        (
            lax.psum_scatter(gain_one_grad, "fsdp", scatter_dimension=0, tiled=True),
            lax.psum_scatter(gain_two_grad, "fsdp", scatter_dimension=0, tiled=True),
            lax.psum_scatter(query_grad, "fsdp", scatter_dimension=0, tiled=True),
            lax.psum_scatter(key_grad, "fsdp", scatter_dimension=0, tiled=True),
            lax.psum_scatter(value_grad, "fsdp", scatter_dimension=0, tiled=True),
            lax.psum_scatter(out_grad, "fsdp", scatter_dimension=0, tiled=True),
            lax.psum_scatter(gate_grad, "fsdp", scatter_dimension=0, tiled=True),
            lax.psum_scatter(up_grad, "fsdp", scatter_dimension=0, tiled=True),
            lax.psum_scatter(down_grad, "fsdp", scatter_dimension=0, tiled=True),
        ),
        "ctx",
    )
    return (output, grad_tokens) + tuple(owned)


def solution(mesh):
    return jax.shard_map(
        body,
        mesh=mesh,
        in_specs=(
            P("fsdp", "ctx", None),
            P(),
            P("fsdp"),
            P("fsdp"),
            P("fsdp", None),
            P("fsdp", None),
            P("fsdp", None),
            P("fsdp", None),
            P("fsdp", None),
            P("fsdp", None),
            P("fsdp", None),
            P("fsdp", "ctx", None),
        ),
        out_specs=(
            P("fsdp", "ctx", None),
            P("fsdp", "ctx", None),
            P("fsdp"),
            P("fsdp"),
            P("fsdp", None),
            P("fsdp", None),
            P("fsdp", None),
            P("fsdp", None),
            P("fsdp", None),
            P("fsdp", None),
            P("fsdp", None),
        ),
        check_vma=False,
    )
```

profile of v0, /device:TPU:0, one launch (start us, length us, event | category | flops | bytes accessed | tf_op | source)
XLA Modules:
  0.0 732.7 jit_solution(17552525240767378965)
XLA Ops:
  11.7 13.5 %all-reduce.7 = (bf16[576]{0:T(1024)(128)(2,1)S(1)}, bf16[576]{0:T(1024)(128)(2,1)S(1)}) all-reduce(bf16[576]{0:T(1024)(128)(2,1)S(1)} %dynamic-update-slice, bf16[576]{0:T(1024)(128)(2,1)S(1)} %dynamic-update-slice.1), channel_id=1, replica_groups=mesh['ctx'=8,'fsdp'=4] {'fsdp'}, use_global_device_ids=true, to_apply=%add | all-reduce | flops 1152 | bytes 4608
  25.3 16.6 %all_gather.51 = bf16[576,192]{1,0:T(8,128)(2,1)S(1)} all-gather(bf16[144,192]{1,0:T(8,128)(2,1)} %param.30), channel_id=1, replica_groups=mesh['ctx'=8,'fsdp'=4] {'fsdp'}, dimensions={0}, use_global_device_ids=true | all-gather | bytes 276480 | tf_op jit(solution)/shard_map/all_gather | solution.py:103
  45.6 16.2 %all_gather.48 = bf16[576,192]{1,0:T(8,128)(2,1)S(1)} all-gather(bf16[144,192]{1,0:T(8,128)(2,1)S(1)} %copy-done.41), channel_id=1, replica_groups=mesh['ctx'=8,'fsdp'=4] {'fsdp'}, dimensions={0}, use_global_device_ids=true | all-gather | bytes 276480 | tf_op jit(solution)/shard_map/all_gather | solution.py:102
  66.5 17.3 %all_gather.50 = bf16[576,576]{1,0:T(8,128)(2,1)S(1)} all-gather(bf16[144,576]{1,0:T(8,128)(2,1)S(1)} %copy-done.34), channel_id=1, replica_groups=mesh['ctx'=8,'fsdp'=4] {'fsdp'}, dimensions={0}, use_global_device_ids=true | all-gather | bytes 829440 | tf_op jit(solution)/shard_map/all_gather | solution.py:101
  86.2 16.3 %all_gather.53 = bf16[576,576]{1,0:T(8,128)(2,1)} all-gather(bf16[144,576]{1,0:T(8,128)(2,1)S(1)} %copy-done.35), channel_id=1, replica_groups=mesh['ctx'=8,'fsdp'=4] {'fsdp'}, dimensions={0}, use_global_device_ids=true | all-gather | bytes 829440 | tf_op jit(solution)/shard_map/all_gather | solution.py:104
  103.1 4.6 fusion.84
  111.3 5.4 all-gather.8.cloned.1.call-done
  116.6 3.0 bitcast_bitcast_fusion
  119.8 58.9 %while.45 = (s32[]{:T(128)}, f32[4,3,3,128]{3,2,1,0:T(4,128)S(1)}, f32[4,3,3,128]{3,2,1,0:T(4,128)S(1)}, f32[4,3,3,128,64]{3,4,2,1,0:T(8,128)S(1)}, s32[128]{0:T...) while((s32[]{:T(128)}, f32[4,3,3,128]{3,2,1,0:T(4,128)S(1)}, ...), condition=%wide.region_9.10_spmd, body=%wide.region_2.9_spmd.sunk | while | flops 159304320 | bytes 10785607 | solution.py:75
  125.2 4.0 conditional.6
  134.6 3.9 conditional.6
  160.1 3.9 conditional.6
  169.4 3.9 conditional.6
  181.5 4.8 fusion.90
  186.3 12.8 %all-gather.12.cloned.1.call-done = bf16[576,1536]{1,0:T(8,128)(2,1)} async-done(((bf16[144,1536]{1,0:T(8,128)(2,1)}), bf16[576,1536]{1,0:T(8,128)(2,1)}) %all-gather.12.cloned.1.call-update) | async-done | bytes 1769488 | tf_op jit(solution)/shard_map/all_gather | solution.py:105
  199.1 6.4 multiply_convert_fusion.1
  218.1 69.0 %while.46 = (s32[]{:T(128)}, f32[4,128,3,3,64]{1,4,3,2,0:T(8,128)}, s32[128]{0:T(128)}, s32[8]{0:T(128)}, s32[16]{0:T(128)}, /*index=5*/bf16[8,4,128,3,64]{2,4,3...) while((s32[]{:T(128)}, f32[4,128,3,3,64]{1,4,3,2,0:T(8,128)}, ...), condition=%wide.region_18.19_spmd, body=%wide.region_13.18_spmd.sunk | while | flops 231253632 | bytes 8934695 | solution.py:75
  224.1 5.2 conditional.7
  225.6 3.7 fusion.29
  235.3 5.2 conditional.7
  236.8 3.7 fusion.29
  264.6 5.3 conditional.7
  266.1 3.8 fusion.29
  275.9 5.2 conditional.7
  277.4 3.7 fusion.29
  293.3 4.4 convolution_bitcast_fusion.3
  299.1 2.8 convolution_bitcast_fusion.2
  303.5 2.8 convolution_bitcast_fusion.1
  307.1 33.8 %all_gather.61 = f32[4,1024,3,3]{1,3,2,0:T(4,128)} all-gather(f32[4,128,3,3]{1,3,2,0:T(4,128)S(1)} %bitcast.317), channel_id=1, replica_groups=mesh['ctx'=8,'fsdp'=4] {'ctx'}, dimensions={1}, use_global_device_ids=true | all-gather | bytes 165888 | tf_op jit(solution)/shard_map/all_gather | solution.py:358
  340.9 9.6 %all_gather.59 = f32[4,1024,3,3]{1,3,2,0:T(4,128)} all-gather(f32[4,128,3,3]{1,3,2,0:T(4,128)S(1)} %bitcast.318), channel_id=1, replica_groups=mesh['ctx'=8,'fsdp'=4] {'ctx'}, dimensions={1}, use_global_device_ids=true | all-gather | bytes 165888 | tf_op jit(solution)/shard_map/all_gather | solution.py:357
  350.5 3.6 copy.66
  354.1 3.4 copy.52
  357.5 3.6 copy.67
  361.1 3.5 copy.53
  365.4 132.0 %while.47 = (s32[]{:T(128)}, f32[4,128,3,64]{1,3,2,0:T(8,128)S(1)}, f32[4,128,3,64]{1,3,2,0:T(8,128)}, s32[8]{0:T(128)}, s32[16]{0:T(128)}, /*index=5*/s32[128]{...) while((s32[]{:T(128)}, f32[4,128,3,64]{1,3,2,0:T(8,128)S(1)}, ...), condition=%wide.region_24.25_spmd, body=%wide.region_19.24_spmd.sunk | while | flops 307046016 | bytes 11558789 | solution.py:75
  371.3 10.5 %conditional.8 = ((f32[4,128,3,64]{1,3,2,0:T(8,128)S(1)}, f32[4,128,3,64]{1,3,2,0:T(8,128)})) conditional(s32[]{:T(128)} %convert_element_type.220, (f32[4,128,3,64]{1,3,2,0:T(8,128)S(1)}, f32[4,128,3,64]{1,3,2,0:T(8,128)}) %tuple.163, (pred[128,128]{1,0:T(8,128)(4,1)}, bf16[8,4,128,3,3,64]{2,5,4,3,1,0:T(8,128)(2,1)}, s32[]{:T(128)}, ...), branch_computations={%region_22.22_spmd, %region_23.23_spmd} | conditional | flops 307003392 | bytes 11538494 | solution.py:346
  377.1 2.5 fusion.61
  379.6 2.3 fusion.58
  387.8 10.6 %conditional.8 = ((f32[4,128,3,64]{1,3,2,0:T(8,128)S(1)}, f32[4,128,3,64]{1,3,2,0:T(8,128)})) conditional(s32[]{:T(128)} %convert_element_type.220, (f32[4,128,3,64]{1,3,2,0:T(8,128)S(1)}, f32[4,128,3,64]{1,3,2,0:T(8,128)}) %tuple.163, (pred[128,128]{1,0:T(8,128)(4,1)}, bf16[8,4,128,3,3,64]{2,5,4,3,1,0:T(8,128)(2,1)}, s32[]{:T(128)}, ...), branch_computations={%region_22.22_spmd, %region_23.23_spmd} | conditional | flops 307003392 | bytes 11538494 | solution.py:346
  391.3 2.3 fusion.55
  393.6 2.5 fusion.61
  396.1 2.3 fusion.58
  404.3 10.5 %conditional.8 = ((f32[4,128,3,64]{1,3,2,0:T(8,128)S(1)}, f32[4,128,3,64]{1,3,2,0:T(8,128)})) conditional(s32[]{:T(128)} %convert_element_type.220, (f32[4,128,3,64]{1,3,2,0:T(8,128)S(1)}, f32[4,128,3,64]{1,3,2,0:T(8,128)}) %tuple.163, (pred[128,128]{1,0:T(8,128)(4,1)}, bf16[8,4,128,3,3,64]{2,5,4,3,1,0:T(8,128)(2,1)}, s32[]{:T(128)}, ...), branch_computations={%region_22.22_spmd, %region_23.23_spmd} | conditional | flops 307003392 | bytes 11538494 | solution.py:346
  410.1 2.5 fusion.61
  420.8 10.5 %conditional.8 = ((f32[4,128,3,64]{1,3,2,0:T(8,128)S(1)}, f32[4,128,3,64]{1,3,2,0:T(8,128)})) conditional(s32[]{:T(128)} %convert_element_type.220, (f32[4,128,3,64]{1,3,2,0:T(8,128)S(1)}, f32[4,128,3,64]{1,3,2,0:T(8,128)}) %tuple.163, (pred[128,128]{1,0:T(8,128)(4,1)}, bf16[8,4,128,3,3,64]{2,5,4,3,1,0:T(8,128)(2,1)}, s32[]{:T(128)}, ...), branch_computations={%region_22.22_spmd, %region_23.23_spmd} | conditional | flops 307003392 | bytes 11538494 | solution.py:346
  426.5 2.5 fusion.61
  429.0 2.3 fusion.58
  437.3 10.5 %conditional.8 = ((f32[4,128,3,64]{1,3,2,0:T(8,128)S(1)}, f32[4,128,3,64]{1,3,2,0:T(8,128)})) conditional(s32[]{:T(128)} %convert_element_type.220, (f32[4,128,3,64]{1,3,2,0:T(8,128)S(1)}, f32[4,128,3,64]{1,3,2,0:T(8,128)}) %tuple.163, (pred[128,128]{1,0:T(8,128)(4,1)}, bf16[8,4,128,3,3,64]{2,5,4,3,1,0:T(8,128)(2,1)}, s32[]{:T(128)}, ...), branch_computations={%region_22.22_spmd, %region_23.23_spmd} | conditional | flops 307003392 | bytes 11538494 | solution.py:346
  443.0 2.5 fusion.61
  453.7 10.8 %conditional.8 = ((f32[4,128,3,64]{1,3,2,0:T(8,128)S(1)}, f32[4,128,3,64]{1,3,2,0:T(8,128)})) conditional(s32[]{:T(128)} %convert_element_type.220, (f32[4,128,3,64]{1,3,2,0:T(8,128)S(1)}, f32[4,128,3,64]{1,3,2,0:T(8,128)}) %tuple.163, (pred[128,128]{1,0:T(8,128)(4,1)}, bf16[8,4,128,3,3,64]{2,5,4,3,1,0:T(8,128)(2,1)}, s32[]{:T(128)}, ...), branch_computations={%region_22.22_spmd, %region_23.23_spmd} | conditional | flops 307003392 | bytes 11538494 | solution.py:346
  459.4 2.8 fusion.61
  470.5 10.5 %conditional.8 = ((f32[4,128,3,64]{1,3,2,0:T(8,128)S(1)}, f32[4,128,3,64]{1,3,2,0:T(8,128)})) conditional(s32[]{:T(128)} %convert_element_type.220, (f32[4,128,3,64]{1,3,2,0:T(8,128)S(1)}, f32[4,128,3,64]{1,3,2,0:T(8,128)}) %tuple.163, (pred[128,128]{1,0:T(8,128)(4,1)}, bf16[8,4,128,3,3,64]{2,5,4,3,1,0:T(8,128)(2,1)}, s32[]{:T(128)}, ...), branch_computations={%region_22.22_spmd, %region_23.23_spmd} | conditional | flops 307003392 | bytes 11538494 | solution.py:346
  476.2 2.5 fusion.61
  487.0 10.4 %conditional.8 = ((f32[4,128,3,64]{1,3,2,0:T(8,128)S(1)}, f32[4,128,3,64]{1,3,2,0:T(8,128)})) conditional(s32[]{:T(128)} %convert_element_type.220, (f32[4,128,3,64]{1,3,2,0:T(8,128)S(1)}, f32[4,128,3,64]{1,3,2,0:T(8,128)}) %tuple.163, (pred[128,128]{1,0:T(8,128)(4,1)}, bf16[8,4,128,3,3,64]{2,5,4,3,1,0:T(8,128)(2,1)}, s32[]{:T(128)}, ...), branch_computations={%region_22.22_spmd, %region_23.23_spmd} | conditional | flops 307003392 | bytes 11538494 | solution.py:346
  492.6 2.5 fusion.61
  495.1 2.3 fusion.58
  503.3 17.2 %reduce-scatter.18.cloned.1.call-done = f32[144,1536]{1,0:T(8,128)} async-done(((f32[576,1536]{1,0:T(8,128)}), f32[144,1536]{1,0:T(8,128)}) %reduce-scatter.18.cloned.1.call-update) | async-done | bytes 884752 | tf_op jit(solution)/shard_map/reduce_scatter | solution.py:411
  520.5 68.8 %reduce-scatter.20.cloned.1.call-done = f32[384,576]{0,1:T(8,128)} async-done(((f32[1536,576]{0,1:T(8,128)}), f32[384,576]{0,1:T(8,128)}) %reduce-scatter.20.cloned.1.call-update) | async-done | bytes 884752 | tf_op jit(solution)/shard_map/reduce_scatter | solution.py:412
  589.4 25.1 %reduce-scatter.10.cloned.1.call-done = f32[144,192]{1,0:T(8,128)} async-done(((f32[576,192]{1,0:T(8,128)}), f32[144,192]{1,0:T(8,128)}) %reduce-scatter.10.cloned.1.call-update) | async-done | bytes 110608 | tf_op jit(solution)/shard_map/reduce_scatter | solution.py:407
  614.5 23.1 %reduce-scatter.12.cloned.1.call-done = f32[144,192]{1,0:T(8,128)} async-done(((f32[576,192]{1,0:T(8,128)}), f32[144,192]{1,0:T(8,128)}) %reduce-scatter.12.cloned.1.call-update) | async-done | bytes 110608 | tf_op jit(solution)/shard_map/reduce_scatter | solution.py:408
  640.1 3.9 fusion.106
  645.7 9.3 %all-reduce.6 = (f32[576]{0:T(1024)S(1)}, f32[576]{0:T(1024)S(1)}) all-reduce(f32[576]{0:T(1024)S(1)} %get-tuple-element.878, f32[576]{0:T(1024)S(1)} %copy-done.49), channel_id=2, replica_groups=mesh['ctx'=8,'fsdp'=4] {'fsdp'}, use_global_device_ids=true, to_apply=%region_27.28.clone | all-reduce | flops 1152 | bytes 9216
  655.1 12.8 %all-reduce.4 = (f32[144]{0:T(256)}, f32[144]{0:T(256)}) all-reduce(f32[144]{0:T(256)S(1)} %dynamic-slice.3, f32[144]{0:T(256)S(1)} %dynamic-slice.5), channel_id=1, replica_groups=mesh['ctx'=8,'fsdp'=4] {'ctx'}, use_global_device_ids=true, to_apply=%region_28.29 | all-reduce | flops 288 | bytes 2304 | tf_op jit(solution)/shard_map/psum | solution.py:402
  669.1 48.4 %all-reduce.10.cloned.1.call-done = (f32[144,576]{1,0:T(8,128)}, f32[144,192]{1,0:T(8,128)}, f32[144,192]{1,0:T(8,128)}, f32[144,576]{1,0:T(8,128)}, f32[144,153...) async-done(((f32[144,576]{1,0:T(8,128)}, f32[144,192]{1,0:T(8,128)}, f32[144,192]{1,0:T(8,128)}, f32[144,576]{1,0:T(8,128)}, f32[144,1536]{1,0:T(8,128)}, ...) | async-done | bytes 3538960 | tf_op jit(solution)/shard_map/psum | solution.py:402
  (387 shorter events, 244.8 us)
Async XLA Ops:
  7.2 38.4 %copy-start.41 = (bf16[144,192]{1,0:T(8,128)(2,1)S(1)}, bf16[144,192]{1,0:T(8,128)(2,1)}, u32[]{:S(2)}) copy-start(bf16[144,192]{1,0:T(8,128)(2,1)} %param.29) | copy-start | bytes 165892
  7.2 95.9 %all-gather.16.cloned.1.call-start = ((), (), s32[]{:S(2)}) async-start(), calls=%async_computation.11 | async-start | bytes 2211840 | tf_op jit(solution)/shard_map/all_gather | solution.py:107
  7.9 99.7 %all-gather.10.cloned.1.call-start = ((), (), s32[]{:S(2)}) async-start(), calls=%async_computation.8 | async-start | bytes 1769472 | tf_op jit(solution)/shard_map/all_gather | solution.py:201
  25.3 58.4 %copy-start.36 = (f32[576]{0:T(1024)}, f32[576]{0:T(1024)S(1)}, u32[]{:S(2)}) copy-start(f32[576]{0:T(1024)S(1)} %convert_element_type.115) | copy-start | bytes 6916
  25.3 38.7 %copy-start.2 = (bf16[4,128,576]{1,2,0:T(8,128)(2,1)S(1)}, bf16[4,128,576]{1,2,0:T(8,128)(2,1)}, u32[]{:S(2)}) copy-start(bf16[4,128,576]{1,2,0:T(8,128)(2,1)} %param.24) | copy-start | bytes 1769476
  41.9 1.3 copy-start.26
  43.3 40.5 %copy-start.42 = (f32[4,128]{1,0:T(4,128)}, f32[4,128]{1,0:T(4,128)S(1)}, u32[]{:S(2)}) copy-start(f32[4,128]{1,0:T(4,128)S(1)} %add_rsqrt_fusion.1) | copy-start | bytes 6148
  45.5 71.1 %all-gather.8.cloned.1.call-start = ((), (), s32[]{:S(2)}) async-start(), calls=%async_computation.7 | async-start | bytes 1769472 | tf_op jit(solution)/shard_map/all_gather | solution.py:200
  61.8 2.2 copy-start.28
  64.0 2.5 copy-start.34
  65.2 116.3 %all-gather.14.cloned.1.call-start = ((), (), s32[]{:S(2)}) async-start(), calls=%async_computation.10 | async-start | bytes 2211840 | tf_op jit(solution)/shard_map/all_gather | solution.py:106
  65.8 133.2 %all-gather.12.cloned.1.call-start = ((), (), s32[]{:S(2)}) async-start(), calls=%async_computation.9 | async-start | bytes 2211840 | tf_op jit(solution)/shard_map/all_gather | solution.py:105
  66.4 284.1 %all-gather.18.cloned.1.call-start = ((), (), s32[]{:S(2)}) async-start(), calls=%async_computation.12 | async-start | bytes 5308416 | tf_op jit(solution)/shard_map/all_gather | solution.py:371
  83.7 0.9 copy-start.10
  84.5 1.7 copy-start.35
  84.7 18.4 %copy-start.18 = (bf16[4,128,576]{1,2,0:T(8,128)(2,1)S(1)}, bf16[4,128,576]{1,2,0:T(8,128)(2,1)}, u32[]{:S(2)}) copy-start(bf16[4,128,576]{1,2,0:T(8,128)(2,1)} %param.35) | copy-start | bytes 1769476
  85.6 272.0 %all-gather.20.cloned.1.call-start = ((), (), s32[]{:S(2)}) async-start(), calls=%async_computation.13 | async-start | bytes 5308416 | tf_op jit(solution)/shard_map/all_gather | solution.py:372
  111.3 8.6 %copy-start.1 = (bf16[4,128,3,3,64]{1,4,3,2,0:T(8,128)(2,1)S(1)}, bf16[4,128,3,3,64]{1,4,3,2,0:T(8,128)(2,1)}, u32[]{:S(2)}) copy-start(bf16[4,128,3,3,64]{1,4,3,2,0:T(8,128)(2,1)} %pad_maximum_fusion) | copy-start | bytes 1769476
  178.8 1.1 copy-start.12
  179.4 1.2 copy-start.14
  179.4 1.9 copy-start.45
  180.6 25.9 %copy-start.7 = (f32[4,128,576]{1,2,0:T(8,128)}, f32[4,128,576]{1,2,0:T(8,128)S(1)}, u32[]{:S(2)}) copy-start(f32[4,128,576]{1,2,0:T(8,128)S(1)} %get-tuple-element.990) | copy-start | bytes 3538948
  181.5 17.6 %copy-start.21 = (bf16[4,128,576]{1,2,0:T(8,128)(2,1)}, bf16[4,128,576]{1,2,0:T(8,128)(2,1)S(1)}, u32[]{:S(2)}) copy-start(bf16[4,128,576]{1,2,0:T(8,128)(2,1)S(1)} %multiply_convert_fusion.3) | copy-start | bytes 1769476
  199.1 6.4 copy-start.25
  205.4 1.2 copy-start.53
  205.4 1.7 copy-start.51
  205.4 1.7 copy-start.46
  205.4 1.7 copy-start.48
  205.5 2.7 copy-start.50
  208.2 2.0 copy-start.19
  210.1 1.7 copy-start.13
  211.8 3.2 copy-start.4
  213.3 4.8 copy-start
  213.3 289.9 %reduce-scatter.8.cloned.1.call-start = ((), (), s32[]{:S(2)}) async-start(), calls=%async_computation.14 | async-start | bytes 1843200 | tf_op jit(solution)/shard_map/reduce_scatter | solution.py:406
  287.1 2.4 copy-start.3
  287.1 2.4 copy-start.37
  287.1 2.4 copy-start.43
  289.5 1.9 copy-start.5
  289.5 1.9 copy-start.15
  291.4 1.9 copy-start.22
  291.4 211.9 %reduce-scatter.14.cloned.1.call-start = ((), (), s32[]{:S(2)}) async-start(), calls=%async_computation.17 | async-start | bytes 1843200 | tf_op jit(solution)/shard_map/reduce_scatter | solution.py:409
  293.3 210.0 %reduce-scatter.16.cloned.1.call-start = ((), (), s32[]{:S(2)}) async-start(), calls=%async_computation.18 | async-start | bytes 4423680 | tf_op jit(solution)/shard_map/reduce_scatter | solution.py:410
  297.7 1.4 copy-start.54
  297.7 222.8 %reduce-scatter.18.cloned.1.call-start = ((), (), s32[]{:S(2)}) async-start(), calls=%async_computation.19 | async-start | bytes 4423680 | tf_op jit(solution)/shard_map/reduce_scatter | solution.py:411
  301.9 1.1 copy-start.20
  301.9 1.6 copy-start.52
  302.0 287.4 %reduce-scatter.20.cloned.1.call-start = ((), (), s32[]{:S(2)}) async-start(), calls=%async_computation.20 | async-start | bytes 4423680 | tf_op jit(solution)/shard_map/reduce_scatter | solution.py:412
  306.4 34.6 %copy-start.40 = (f32[4,3,3,128]{3,2,1,0:T(4,128)S(1)}, f32[4,3,3,128]{3,2,1,0:T(4,128)}, u32[]{:S(2)}) copy-start(f32[4,3,3,128]{3,2,1,0:T(4,128)} %get-tuple-element.1441) | copy-start | bytes 55300
  306.4 308.1 %reduce-scatter.10.cloned.1.call-start = ((), (), s32[]{:S(2)}) async-start(), calls=%async_computation.15 | async-start | bytes 737280 | tf_op jit(solution)/shard_map/reduce_scatter | solution.py:407
  361.1 4.3 copy-start.9
  498.2 3.1 copy-start.38
  498.2 3.1 copy-start.44
  500.2 137.4 %reduce-scatter.12.cloned.1.call-start = ((), (), s32[]{:S(2)}) async-start(), calls=%async_computation.16 | async-start | bytes 737280 | tf_op jit(solution)/shard_map/reduce_scatter | solution.py:408
  502.5 215.1 %all-reduce.10.cloned.1.call-start = ((), (), s32[]{:S(2)}) async-start(), calls=%async_computation.21 | async-start | bytes 7372800 | tf_op jit(solution)/shard_map/psum | solution.py:402
  637.6 1.1 copy-start.11
  637.6 1.3 copy-start.17
  638.8 1.3 copy-start.8
  640.1 3.9 copy-start.29
  644.0 1.0 copy-start.27
  645.0 23.0 %copy-start.6 = (f32[4,128,576]{1,2,0:T(8,128)S(1)}, f32[4,128,576]{1,2,0:T(8,128)}, u32[]{:S(2)}) copy-start(f32[4,128,576]{1,2,0:T(8,128)} %copy-done.4) | copy-start | bytes 3538948
  717.6 5.1 copy-start.33
  717.6 5.8 copy-start.32
  719.4 4.9 copy-start.31
  723.4 1.8 copy-start.30
  (6 other events, 4.1 us)
Sparse Core Ops, SparseCore 0:
  9.6 52.3 all-gather.15
  63.9 24.8 all-gather.9
  90.7 25.8 all-gather.7
  118.1 40.3 all-gather.13
  159.8 39.1 all-gather.11
  201.4 38.6 all-gather.17
  242.5 39.7 all-gather.19
  291.5 57.3 reduce-scatter.7
  351.4 32.6 reduce-scatter.13
  386.2 65.2 reduce-scatter.15
  453.8 66.6 reduce-scatter.17
  522.7 66.6 reduce-scatter.19
  592.2 22.1 reduce-scatter.9
  617.2 20.2 reduce-scatter.11
  641.6 75.8 all-reduce.9
where the time goes:
time: 737 us; the launch traced here: 733 us
  waiting for transfers between devices  203 us (28%)
  blocking collectives  146 us (20%)
  matrix products  137 us (19%)
  other arithmetic  112 us (15%)
  local copies, waits for them, and re-layouts  86.9 us (12%)
  loops' own time  32.2 us (4%)
  between operations  15.9 us (2%)
    reduce_scatter x1, waiting for transfers between devices, body(): lax.psum_scatter(down_grad, 'fsdp', scatter_dimension=0, tiled=True)  68.8 us
    psum x1, waiting for transfers between devices, body(): lax.psum((lax.psum_scatter(gain_one_grad, 'fsdp', scatter_dimension=0, ti...  48.4 us
    all_gather x1, blocking collectives, body(): lax.all_gather(row_delta, 'ctx', axis=1, tiled=True)  33.8 us
    unnamed x127, local copies, waits for them, and re-layouts  31.3 us
    dynamic_slice x24, local copies, waits for them, and re-layouts, blockwise(): result, unused = lax.scan(scan_step, carried, (offsets, stacked))  29.8 us
    reduce_scatter x1, waiting for transfers between devices, body(): lax.psum_scatter(key_grad, 'fsdp', scatter_dimension=0, tiled=True)  25.1 us
    reduce_scatter x1, waiting for transfers between devices, body(): lax.psum_scatter(value_grad, 'fsdp', scatter_dimension=0, tiled=True)  23.1 us
    unnamed x2, blocking collectives  22.8 us
  transfers between devices with their start and end apart: 15, of which 7 were waited for; matrix products, arithmetic and copies ran while one was open for 43% of the time, Pallas kernels for 0%

commit v1 on v0

v1 whole, which is shorter than its diff:
```python
import functools
import math

import jax
import jax.numpy as jnp
from jax import lax
from jax.experimental import pallas as pl
from jax.experimental.pallas import tpu as pltpu
from jax.sharding import PartitionSpec as P

QUERY_HEADS = 9
KEY_VALUE_HEADS = 3
HEAD_DIMENSION = 64


eps = 1e-05
rope_base = 100000.0
mask_fill_value = -1e30


def row_positions(row_ids, block_order, half_size):
    slot_ids = jnp.arange(block_order.shape[0], dtype=jnp.int32)
    chosen = jnp.sum(
        jnp.where((row_ids // half_size)[:, None] == slot_ids[None, :], block_order[None, :], 0),
        axis=1,
    )
    return chosen * half_size + row_ids % half_size


def rope_tables(token_positions):
    inverse = jnp.exp(
        jnp.arange(HEAD_DIMENSION // 2, dtype=jnp.float32)
        * (-2.0 * math.log(rope_base) / HEAD_DIMENSION)
    )
    angles = token_positions.astype(jnp.float32)[:, None] * inverse[None, :]
    return (jnp.cos(angles), jnp.sin(angles))


def apply_rotary(vectors, cosine_table, sine_table):
    front = vectors[..., : HEAD_DIMENSION // 2]
    back_half = vectors[..., HEAD_DIMENSION // 2 :]
    cos_rows = cosine_table[:, None, :]
    sin_rows = sine_table[:, None, :]
    return jnp.concatenate(
        [front * cos_rows - back_half * sin_rows, back_half * cos_rows + front * sin_rows], axis=-1
    )


def rms_scale(values_in):
    return lax.rsqrt(jnp.mean(values_in * values_in, axis=-1, keepdims=True) + eps)


def norm_back(grad_normed, base_rows, gain_rows, scale_rows):
    scaled = grad_normed * gain_rows
    return scale_rows * (scaled - base_rows * jnp.mean(scaled * base_rows, axis=-1, keepdims=True))


def chunk_rows(count):
    return 1024 if count % 1024 == 0 else count


def run_chunks(count, step_fn, carried):
    if count == 1:
        return step_fn(0, carried)
    return lax.fori_loop(0, count, step_fn, carried)


def heads_row(transposed, group):
    width = HEAD_DIMENSION
    return jnp.concatenate(
        [transposed[(group * 3 + g) * width : (group * 3 + g + 1) * width] for g in range(3)],
        axis=1,
    )


def forward_kernel(q_ref, kv_ref, qpos_ref, kpos_ref, mixed_ref, lse_ref, out_scr):
    rows = q_ref.shape[1]
    keys = kv_ref.shape[1]
    width = HEAD_DIMENSION
    size = chunk_rows(keys)
    q_all = q_ref[0].astype(jnp.float32).T.astype(jnp.bfloat16)
    qpos = qpos_ref[...]
    qpos3 = jnp.concatenate([qpos, qpos, qpos], axis=1)
    for group in range(KEY_VALUE_HEADS):
        qt = heads_row(q_all, group)

        def step(c, carried):
            start = c * size
            k = kv_ref[0, pl.ds(start, size), group * width : (group + 1) * width]
            v = kv_ref[0, pl.ds(start, size), (3 + group) * width : (4 + group) * width]
            allowed = kpos_ref[pl.ds(start, size), :] <= qpos3
            scores = jnp.dot(k, qt, preferred_element_type=jnp.float32)
            masked = jnp.where(allowed, scores, mask_fill_value)
            top, total, accum = carried
            new_top = jnp.maximum(top, jnp.max(masked, axis=0, keepdims=True))
            exponent = jnp.exp(masked - new_top)
            factor = jnp.exp(top - new_top)
            part = lax.dot_general(
                v,
                exponent.astype(jnp.bfloat16),
                (((0,), (0,)), ((), ())),
                preferred_element_type=jnp.float32,
            )
            return (
                new_top,
                total * factor + jnp.sum(exponent, axis=0, keepdims=True),
                accum * factor + part,
            )

        top, total, accum = run_chunks(
            keys // size,
            step,
            (
                jnp.full((1, 3 * rows), mask_fill_value, jnp.float32),
                jnp.zeros((1, 3 * rows), jnp.float32),
                jnp.zeros((width, 3 * rows), jnp.float32),
            ),
        )
        attended = accum / total
        lse = top + jnp.log(total)
        for g in range(3):
            head = group * 3 + g
            out_scr[head * width : (head + 1) * width, :] = attended[:, g * rows : (g + 1) * rows]
            lse_ref[0, head : head + 1, :] = lse[:, g * rows : (g + 1) * rows]
    mixed_ref[0] = out_scr[...].T.astype(jnp.bfloat16)


def backward_kernel(
    q_ref, kv_ref, do_ref, mixed_ref, lse_ref, qpos_ref, kpos_ref, dq_ref, dkv_ref, dq_scr
):
    rows = q_ref.shape[1]
    keys = kv_ref.shape[1]
    width = HEAD_DIMENSION
    size = chunk_rows(keys)
    q_rows = q_ref[0]
    do_rows = do_ref[0]
    q_all = q_rows.astype(jnp.float32).T.astype(jnp.bfloat16)
    do_wide = do_rows.astype(jnp.float32).T
    do_all = do_wide.astype(jnp.bfloat16)
    product = do_wide * mixed_ref[0].astype(jnp.float32).T
    qpos = qpos_ref[...]
    qpos3 = jnp.concatenate([qpos, qpos, qpos], axis=1)
    for group in range(KEY_VALUE_HEADS):
        qt = heads_row(q_all, group)
        dot = heads_row(do_all, group)
        delta = jnp.sum(heads_row(product, group), axis=0, keepdims=True)
        lse = jnp.concatenate(
            [lse_ref[0, group * 3 + g : group * 3 + g + 1, :] for g in range(3)], axis=1
        )
        first = group * 3 * width
        q = jnp.concatenate(
            [q_rows[:, first + g * width : first + (g + 1) * width] for g in range(3)], axis=0
        )
        do = jnp.concatenate(
            [do_rows[:, first + g * width : first + (g + 1) * width] for g in range(3)], axis=0
        )

        def step(c, dq):
            start = c * size
            k = kv_ref[0, pl.ds(start, size), group * width : (group + 1) * width]
            v = kv_ref[0, pl.ds(start, size), (3 + group) * width : (4 + group) * width]
            allowed = kpos_ref[pl.ds(start, size), :] <= qpos3
            scores = jnp.dot(k, qt, preferred_element_type=jnp.float32)
            p = jnp.exp(jnp.where(allowed, scores - lse, mask_fill_value))
            dp = jnp.dot(v, dot, preferred_element_type=jnp.float32)
            ds = (p * (dp - delta)).astype(jnp.bfloat16)
            dkv_ref[0, pl.ds(start, size), (3 + group) * width : (4 + group) * width] = jnp.dot(
                p.astype(jnp.bfloat16), do, preferred_element_type=jnp.float32
            ).astype(jnp.bfloat16)
            dkv_ref[0, pl.ds(start, size), group * width : (group + 1) * width] = jnp.dot(
                ds, q, preferred_element_type=jnp.float32
            ).astype(jnp.bfloat16)
            return dq + lax.dot_general(
                k, ds, (((0,), (0,)), ((), ())), preferred_element_type=jnp.float32
            )

        dq = run_chunks(keys // size, step, jnp.zeros((width, 3 * rows), jnp.float32))
        for g in range(3):
            head = group * 3 + g
            dq_scr[head * width : (head + 1) * width, :] = dq[:, g * rows : (g + 1) * rows]
    dq_ref[0] = dq_scr[...].T


def seq_spec(rows, columns):
    return pl.BlockSpec((1, rows, columns), lambda s: (s, 0, 0))


def flat_spec(rows, columns):
    return pl.BlockSpec((rows, columns), lambda s: (0, 0))


def attend(q, kv, qpos, kpos):
    seqs, rows, wide = q.shape
    keys, both = kv.shape[1:]
    return pl.pallas_call(
        forward_kernel,
        grid=(seqs,),
        in_specs=[seq_spec(rows, wide), seq_spec(keys, both), flat_spec(1, rows), flat_spec(keys, 1)],
        out_specs=[seq_spec(rows, wide), seq_spec(16, rows)],
        out_shape=[
            jax.ShapeDtypeStruct((seqs, rows, wide), jnp.bfloat16),
            jax.ShapeDtypeStruct((seqs, 16, rows), jnp.float32),
        ],
        scratch_shapes=[pltpu.VMEM((wide, rows), jnp.float32)],
        compiler_params=pltpu.CompilerParams(vmem_limit_bytes=56 << 20),
        cost_estimate=pl.CostEstimate(
            flops=4 * seqs * rows * wide * keys * 3, bytes_accessed=kv.size * 2, transcendentals=0
        ),
    )(q, kv, qpos, kpos)


def attend_back(q, kv, grad, mixed, lse, qpos, kpos):
    seqs, rows, wide = q.shape
    keys, both = kv.shape[1:]
    return pl.pallas_call(
        backward_kernel,
        grid=(seqs,),
        in_specs=[
            seq_spec(rows, wide),
            seq_spec(keys, both),
            seq_spec(rows, wide),
            seq_spec(rows, wide),
            seq_spec(16, rows),
            flat_spec(1, rows),
            flat_spec(keys, 1),
        ],
        out_specs=[seq_spec(rows, wide), seq_spec(keys, both)],
        out_shape=[
            jax.ShapeDtypeStruct((seqs, rows, wide), jnp.float32),
            jax.ShapeDtypeStruct((seqs, keys, both), jnp.bfloat16),
        ],
        scratch_shapes=[pltpu.VMEM((wide, rows), jnp.float32)],
        compiler_params=pltpu.CompilerParams(vmem_limit_bytes=56 << 20),
        cost_estimate=pl.CostEstimate(
            flops=10 * seqs * rows * wide * keys * 3, bytes_accessed=kv.size * 4, transcendentals=0
        ),
    )(q, kv, grad, mixed, lse, qpos, kpos)


def exchange_kernel(axis, count, source, target, x_ref, o_ref, send_sem, recv_sem, local_sem):
    me = lax.axis_index(axis)
    barrier = pltpu.get_barrier_semaphore()
    for hop in range(1, count):
        pl.semaphore_signal(
            barrier,
            inc=1,
            device_id={axis: lax.rem(me + hop, count)},
            device_id_type=pl.DeviceIdType.MESH,
        )
    own = pltpu.make_async_copy(source(x_ref, me), target(o_ref, me), local_sem)
    own.start()
    pl.semaphore_wait(barrier, count - 1)
    copies = []
    for hop in range(1, count):
        peer = lax.rem(me + hop, count)
        copy = pltpu.make_async_remote_copy(
            src_ref=source(x_ref, peer),
            dst_ref=target(o_ref, me),
            send_sem=send_sem.at[hop],
            recv_sem=recv_sem.at[hop],
            device_id={axis: peer},
            device_id_type=pl.DeviceIdType.MESH,
        )
        copy.start()
        copies.append(copy)
    own.wait()
    for copy in copies:
        copy.wait()


def exchange(x, axis, count, source, target, out_dims, collective_id):
    return pl.pallas_call(
        functools.partial(exchange_kernel, axis, count, source, target),
        in_specs=[pl.BlockSpec(memory_space=pl.ANY)],
        out_specs=pl.BlockSpec(memory_space=pl.ANY),
        out_shape=jax.ShapeDtypeStruct(out_dims, x.dtype),
        scratch_shapes=[
            pltpu.SemaphoreType.DMA((count,)),
            pltpu.SemaphoreType.DMA((count,)),
            pltpu.SemaphoreType.DMA,
        ],
        compiler_params=pltpu.CompilerParams(collective_id=collective_id, has_side_effects=True),
    )(x)


def gather_rows(x, axis, collective_id):
    count, rows = lax.axis_size(axis), x.shape[0]
    return exchange(
        x,
        axis,
        count,
        lambda ref, peer: ref,
        lambda ref, me: ref.at[pl.ds(pl.multiple_of(me * rows, 16), rows)],
        (count * rows,) + x.shape[1:],
        collective_id,
    )


def gather_keys(x, collective_id):
    count, rows = lax.axis_size("ctx"), x.shape[1]
    return exchange(
        x,
        "ctx",
        count,
        lambda ref, peer: ref,
        lambda ref, me: ref.at[:, pl.ds(pl.multiple_of(me * rows, 16), rows)],
        (x.shape[0], count * rows, x.shape[2]),
        collective_id,
    )


def reduce_keys(x, collective_id):
    count = lax.axis_size("ctx")
    rows = x.shape[1] // count
    parts = exchange(
        x,
        "ctx",
        count,
        lambda ref, peer: ref.at[:, pl.ds(pl.multiple_of(peer * rows, 16), rows)],
        lambda ref, me: ref.at[me],
        (count, x.shape[0], rows, x.shape[2]),
        collective_id,
    )
    return jnp.sum(parts.astype(jnp.float32), axis=0)


def gather_shares(x):
    count, rows = lax.axis_size("ctx"), x.shape[0]
    if rows % count:
        return lax.all_gather(x, "fsdp", axis=0, tiled=True)
    share = lax.dynamic_slice_in_dim(x, lax.axis_index("ctx") * (rows // count), rows // count, 0)
    along = lax.all_gather(share, "fsdp", axis=0, tiled=False)
    whole = lax.all_gather(along, "ctx", axis=1, tiled=False)
    return whole.reshape((-1,) + x.shape[1:])


def reduce_rows(x):
    count, parts = lax.axis_size("ctx"), lax.axis_size("fsdp")
    rows = x.shape[0] // parts
    x = x.astype(jnp.bfloat16)
    if rows % count:
        return lax.psum(
            lax.psum_scatter(x, "fsdp", scatter_dimension=0, tiled=True), "ctx"
        ).astype(jnp.float32)
    x = x.reshape((parts, count, rows // count) + x.shape[1:])
    x = lax.psum_scatter(x, "ctx", scatter_dimension=1, tiled=False)
    x = lax.psum_scatter(x, "fsdp", scatter_dimension=0, tiled=False)
    return lax.all_gather(x, "ctx", axis=0, tiled=True).astype(jnp.float32)

def body(
    tokens,
    block_order,
    gain_one,
    gain_two,
    query_weight,
    key_matrix,
    value_matrix,
    out_weight,
    gate_weight,
    up_weight,
    down_weight,
    cotangent,
):
    count_of_sequences, rows_per_block, model_width = tokens.shape
    half_size = rows_per_block // 2
    score_scale = HEAD_DIMENSION ** (-0.5)
    ctx_index = lax.axis_index("ctx")
    first_pack = gather_rows(
        jnp.concatenate([query_weight, key_matrix, value_matrix], axis=1), "fsdp", 0
    )
    kv_width = KEY_VALUE_HEADS * HEAD_DIMENSION
    query_width = query_weight.shape[1]
    ff_width = gate_weight.shape[1]
    gains = lax.all_gather(jnp.stack([gain_one, gain_two]), "fsdp", axis=1, tiled=True)
    second_pack = gather_shares(jnp.concatenate([out_weight, gate_weight, up_weight], axis=1))
    gathered = (
        gains[0],
        gains[1],
        first_pack[:, :query_width],
        first_pack[:, query_width : query_width + kv_width],
        first_pack[:, query_width + kv_width :],
        second_pack[:, :model_width],
        second_pack[:, model_width : model_width + ff_width],
        second_pack[:, model_width + ff_width :],
        gather_shares(down_weight),
    )
    gain_first = gathered[0].astype(jnp.float32)
    gain_second = gathered[1].astype(jnp.float32)
    query_full, key_full, value_full, out_full, gate_full, up_full, down_full = gathered[2:]
    own_positions = row_positions(
        ctx_index * rows_per_block + jnp.arange(rows_per_block, dtype=jnp.int32),
        block_order,
        half_size,
    )
    cosine_table, sine_table = rope_tables(own_positions)
    inputs = tokens.astype(jnp.float32)
    scale_one = rms_scale(inputs)
    base_one = inputs * scale_one
    normed = (base_one * gain_first).astype(jnp.bfloat16)
    query_rows_all = jnp.dot(normed, query_full, preferred_element_type=jnp.float32).reshape(
        count_of_sequences, rows_per_block, QUERY_HEADS, HEAD_DIMENSION
    )
    projected_key = jnp.dot(normed, key_full, preferred_element_type=jnp.float32).reshape(
        count_of_sequences, rows_per_block, KEY_VALUE_HEADS, HEAD_DIMENSION
    )
    projected_value = jnp.dot(normed, value_full, preferred_element_type=jnp.float32).astype(
        jnp.bfloat16
    )
    scaled_query = (
        (apply_rotary(query_rows_all, cosine_table, sine_table).astype(jnp.bfloat16) * score_scale)
        .astype(jnp.bfloat16)
        .reshape(count_of_sequences, rows_per_block, QUERY_HEADS * HEAD_DIMENSION)
    )
    rotary_key = (
        apply_rotary(projected_key, cosine_table, sine_table)
        .astype(jnp.bfloat16)
        .reshape(count_of_sequences, rows_per_block, KEY_VALUE_HEADS * HEAD_DIMENSION)
    )
    key_value = gather_keys(jnp.concatenate([rotary_key, projected_value], axis=-1), 1)
    key_positions = row_positions(
        jnp.arange(key_value.shape[1], dtype=jnp.int32), block_order, half_size
    )[:, None]
    query_positions = own_positions[None, :]
    mixed_heads, log_total = attend(scaled_query, key_value, query_positions, key_positions)
    middle = inputs + jnp.dot(mixed_heads, out_full, preferred_element_type=jnp.float32)
    scale_two = rms_scale(middle)
    base_two = middle * scale_two
    normed_two = (base_two * gain_second).astype(jnp.bfloat16)
    gate_proj = jnp.dot(normed_two, gate_full, preferred_element_type=jnp.float32)
    up_proj = jnp.dot(normed_two, up_full, preferred_element_type=jnp.float32)
    sigmoid_gate = jax.nn.sigmoid(gate_proj)
    activated = gate_proj * sigmoid_gate
    hidden = (activated * up_proj).astype(jnp.bfloat16)
    output = (middle + jnp.dot(hidden, down_full, preferred_element_type=jnp.float32)).astype(
        jnp.bfloat16
    )
    down_grad = jnp.einsum("sbf,sbd->fd", hidden, cotangent, preferred_element_type=jnp.float32)
    grad_hidden = jnp.einsum(
        "sbd,fd->sbf", cotangent, down_full, preferred_element_type=jnp.float32
    )
    grad_gate = (
        grad_hidden * up_proj * sigmoid_gate * (1.0 + gate_proj * (1.0 - sigmoid_gate))
    ).astype(jnp.bfloat16)
    grad_up = (grad_hidden * activated).astype(jnp.bfloat16)
    gate_grad = jnp.einsum("sbd,sbf->df", normed_two, grad_gate, preferred_element_type=jnp.float32)
    up_grad = jnp.einsum("sbd,sbf->df", normed_two, grad_up, preferred_element_type=jnp.float32)
    grad_normed_two = jnp.einsum(
        "sbf,df->sbd", grad_gate, gate_full, preferred_element_type=jnp.float32
    ) + jnp.einsum("sbf,df->sbd", grad_up, up_full, preferred_element_type=jnp.float32)
    gain_two_grad = jnp.sum(grad_normed_two * base_two, axis=(0, 1))
    grad_middle = cotangent.astype(jnp.float32) + norm_back(
        grad_normed_two, base_two, gain_second, scale_two
    )
    grad_branch = grad_middle.astype(jnp.bfloat16)
    out_grad = jnp.einsum(
        "sbq,sbd->qd", mixed_heads, grad_branch, preferred_element_type=jnp.float32
    )
    mixed_gradient = jnp.einsum(
        "sbd,qd->sbq", grad_branch, out_full, preferred_element_type=jnp.float32
    ).astype(jnp.bfloat16)
    owned_down = reduce_rows(down_grad)
    owned_early = reduce_rows(
        jnp.concatenate([out_grad, gate_grad, up_grad, gain_two_grad[:, None]], axis=1)
    )
    query_sum, key_value_part = attend_back(
        scaled_query,
        key_value,
        mixed_gradient,
        mixed_heads,
        log_total,
        query_positions,
        key_positions,
    )
    query_sum = query_sum * score_scale
    grad_query = (
        apply_rotary(
            query_sum.reshape(count_of_sequences, rows_per_block, QUERY_HEADS, HEAD_DIMENSION),
            cosine_table,
            -sine_table,
        )
        .astype(jnp.bfloat16)
        .reshape(count_of_sequences, rows_per_block, QUERY_HEADS * HEAD_DIMENSION)
    )

    key_value_sum = reduce_keys(key_value_part, 2)
    key_sum = key_value_sum[..., :kv_width].reshape(
        count_of_sequences, rows_per_block, KEY_VALUE_HEADS, HEAD_DIMENSION
    )
    grad_key = (
        apply_rotary(key_sum, cosine_table, -sine_table)
        .astype(jnp.bfloat16)
        .reshape(count_of_sequences, rows_per_block, kv_width)
    )
    value_gradient = key_value_sum[..., kv_width:].astype(jnp.bfloat16)
    query_grad = jnp.einsum("sbd,sbq->dq", normed, grad_query, preferred_element_type=jnp.float32)
    key_grad = jnp.einsum("sbd,sbq->dq", normed, grad_key, preferred_element_type=jnp.float32)
    value_grad = jnp.einsum(
        "sbd,sbq->dq", normed, value_gradient, preferred_element_type=jnp.float32
    )
    grad_normed = jnp.einsum(
        "sbq,dq->sbd", grad_query, query_full, preferred_element_type=jnp.float32
    )
    grad_normed = grad_normed + jnp.einsum(
        "sbq,dq->sbd", grad_key, key_full, preferred_element_type=jnp.float32
    )
    grad_normed = grad_normed + jnp.einsum(
        "sbq,dq->sbd", value_gradient, value_full, preferred_element_type=jnp.float32
    )
    gain_one_grad = jnp.sum(grad_normed * base_one, axis=(0, 1))
    grad_tokens = (grad_middle + norm_back(grad_normed, base_one, gain_first, scale_one)).astype(
        jnp.bfloat16
    )
    owned_late = reduce_rows(
        jnp.concatenate([query_grad, key_grad, value_grad, gain_one_grad[:, None]], axis=1)
    )
    owned = (
        owned_late[:, -1],
        owned_early[:, -1],
        owned_late[:, :query_width],
        owned_late[:, query_width : query_width + kv_width],
        owned_late[:, query_width + kv_width : query_width + 2 * kv_width],
        owned_early[:, :model_width],
        owned_early[:, model_width : model_width + ff_width],
        owned_early[:, model_width + ff_width : model_width + 2 * ff_width],
        owned_down,
    )
    return (output, grad_tokens) + tuple(owned)


def solution(mesh):
    return jax.shard_map(
        body,
        mesh=mesh,
        in_specs=(
            P("fsdp", "ctx", None),
            P(),
            P("fsdp"),
            P("fsdp"),
            P("fsdp", None),
            P("fsdp", None),
            P("fsdp", None),
            P("fsdp", None),
            P("fsdp", None),
            P("fsdp", None),
            P("fsdp", None),
            P("fsdp", "ctx", None),
        ),
        out_specs=(
            P("fsdp", "ctx", None),
            P("fsdp", "ctx", None),
            P("fsdp"),
            P("fsdp"),
            P("fsdp", None),
            P("fsdp", None),
            P("fsdp", None),
            P("fsdp", None),
            P("fsdp", None),
            P("fsdp", None),
            P("fsdp", None),
        ),
        check_vma=False,
    )
```

time: 737 us -> 527 us (0.72)
  Pallas kernels: 0 us -> 125 us
  other arithmetic: 112 us -> 14.5 us
  matrix products: 137 us -> 41.6 us
  blocking collectives: 146 us -> 69.8 us
  loops' own time: 32.2 us -> 0 us
  waiting for transfers between devices: 203 us -> 174 us
    unnamed x15 -> x9, waiting for transfers between devices: 1.93 us -> 135 us
    pallas_call x0 -> x5, Pallas kernels: none -> 125 us  [the longest x3 95.7 us: exchange(): pl.pallas_call(functools.partial(exchange_kernel, axis, count, source, ta...]
    reduce_scatter x7 -> x2, waiting for transfers between devices: 134 us -> 20.8 us  [reduce_rows(): x = lax.psum_scatter(x, 'fsdp', scatter_dimension=0, tiled=False)]
    dot_general x40 -> x0, matrix products: 90.2 us -> none  [the longest x8 20.4 us: key_compute(): jnp.einsum('shgnb,snhgd->sbhd', grad_score, far_queries, preferred_elemen...]
    psum x1 -> x0, waiting for transfers between devices: 48.4 us -> none  [body(): lax.psum((lax.psum_scatter(gain_one_grad, 'fsdp', scatter_dimension=0, ti...]
    ge x24 -> x0, other arithmetic: 43.7 us -> none  [the longest x8 16.4 us: query_block(): own_positions[:, None] >= far_rows(first_row, far_keys.shape[1])[None, :]]
    all_gather x6 -> x5, blocking collectives: 110 us -> 69.8 us  [the longest x2 35.1 us: gather_shares(): along = lax.all_gather(share, 'fsdp', axis=0, tiled=False)]
    concatenate x0 -> x10, local copies, waits for them, and re-layouts: none -> 35.6 us  [the longest x6 29 us: body(): jnp.concatenate([out_grad, gate_grad, up_grad, gain_two_grad[:, None]], a...]
  transfers between devices with their start and end apart: 15 -> 7, of which waited for: 7 -> 5; matrix products, arithmetic and copies ran while one was open for 43% -> 7% of each run, Pallas kernels for 0% -> 14%
where the time goes in v1:
time: 527 us; the launch traced here: 520 us
  waiting for transfers between devices  174 us (33%)
  Pallas kernels  125 us (24%)
  local copies, waits for them, and re-layouts  79.9 us (15%)
  blocking collectives  69.8 us (13%)
  matrix products  41.6 us (8%)
  between operations  15.2 us (3%)
  other arithmetic  14.5 us (3%)
    unnamed x9, waiting for transfers between devices  135 us
    pallas_call x3, Pallas kernels, exchange(): pl.pallas_call(functools.partial(exchange_kernel, axis, count, source, ta...  95.7 us
    all_gather x2, blocking collectives, gather_shares(): along = lax.all_gather(share, 'fsdp', axis=0, tiled=False)  35.1 us
    concatenate x6, local copies, waits for them, and re-layouts, body(): jnp.concatenate([out_grad, gate_grad, up_grad, gain_two_grad[:, None]], a...  29 us
    reduce_scatter x2, waiting for transfers between devices, reduce_rows(): x = lax.psum_scatter(x, 'fsdp', scatter_dimension=0, tiled=False)  20.8 us
    all_gather x2, blocking collectives, reduce_rows(): return lax.all_gather(x, 'ctx', axis=0, tiled=True).astype(jnp.float32)  20 us
    all_gather x1, waiting for transfers between devices, reduce_rows(): return lax.all_gather(x, 'ctx', axis=0, tiled=True).astype(jnp.float32)  17.5 us
    pallas_call x1, Pallas kernels, attend_back(): pl.pallas_call(backward_kernel, grid=(seqs,), in_specs=[seq_spec(rows, wi...  16.6 us
  transfers between devices with their start and end apart: 7, of which 5 were waited for; matrix products, arithmetic and copies ran while one was open for 7% of the time, Pallas kernels for 14%

profile of v1, /device:TPU:0, one launch (start us, length us, event | category | flops | bytes accessed | tf_op | source)
XLA Modules:
  0.0 519.7 jit_solution(17937437505023562362)
XLA Ops:
  7.2 2.6 concatenate.51
  10.0 20.5 %all-gather.8 = bf16[4,18,3648]{2,1,0:T(8,128)(2,1)S(1)} all-gather(bf16[1,18,3648]{2,1,0:T(8,128)(2,1)S(1)} %dynamic-slice_bitcast_fusion.2), channel_id=2, replica_groups=mesh['ctx'=8,'fsdp'=4] {'fsdp'}, dimensions={0}, use_global_device_ids=true | all-gather | bytes 656640 | tf_op jit(solution)/shard_map/all_gather | solution.py:332
  30.4 1.0 copy.265
  31.8 14.6 %all-gather.2 = bf16[192,576]{1,0:T(8,128)(2,1)} all-gather(bf16[48,576]{1,0:T(8,128)(2,1)S(1)} %copy.320), channel_id=4, replica_groups=mesh['ctx'=8,'fsdp'=4] {'fsdp'}, dimensions={0}, use_global_device_ids=true | all-gather | bytes 276480 | tf_op jit(solution)/shard_map/all_gather | solution.py:332
  47.3 18.4 %shard_map.203 = bf16[576,960]{1,0:T(8,128)(2,1)} custom-call(bf16[144,960]{1,0:T(8,128)(2,1)} %pad_maximum_fusion.3.x_ref), custom_call_target="tpu_custom_call" | custom-call | tf_op jit(solution)/shard_map/pallas_call | solution.py:272
  65.8 14.7 %all-gather.7 = bf16[4,144,2]{1,2,0:T(2,128)(2,1)S(1)} all-gather(bf16[1,144,2]{1,2,0:T(2,128)(2,1)S(1)} %maximum_bitcast_fusion), channel_id=1, replica_groups=mesh['ctx'=8,'fsdp'=4] {'fsdp'}, dimensions={0}, use_global_device_ids=true | all-gather | bytes 2880 | tf_op jit(solution)/shard_map/all_gather | solution.py:374
  80.7 1.9 fusion.25
  82.7 1.1 convolution_convert_fusion.1
  83.8 1.4 fusion.36
  86.5 1.1 copy.264.q_ref
  88.8 39.5 %shard_map.204.kv_ref = bf16[4,1024,384]{2,1,0:T(8,128)(2,1)} custom-call(bf16[4,128,384]{2,1,0:T(8,128)(2,1)} %pad_maximum_fusion.2.x_ref), custom_call_target="tpu_custom_call" | custom-call | tf_op jit(solution)/shard_map/pallas_call | solution.py:272
  130.0 12.5 %shard_map.205 = (bf16[4,128,576]{2,1,0:T(8,128)(2,1)}, f32[4,16,128]{2,1,0:T(8,128)}) custom-call(bf16[4,128,576]{2,1,0:T(8,128)(2,1)} %copy.264.q_ref, bf16[4,1024,384]{2,1,0:T(8,128)(2,1)} %shard_map.204.kv_ref, s32[1,128]{1,0:T(1,128)} %fusion.53.qpos_ref, s32[1024,1]{1,0:T(8,128)} %fusion.29.kpos_ref), custom_call_target="tpu_custom_call" | custom-call | flops 3623878656 | bytes 3145728 | tf_op jit(solution)/shard_map/pallas_call | solution.py:195
  142.5 2.7 copy.266
  146.2 3.2 fusion.6
  149.4 3.2 fusion.8
  152.6 7.6 %multiply_convert_fusion = (bf16[4,128,1536]{2,1,0:T(8,128)(2,1)S(1)}, bf16[4,128,1536]{2,1,0:T(8,128)(2,1)S(1)}, bf16[4,128,1536]{2,1,0:T(8,128)(2,1)}) fusion(f32[4,128,1536]{2,1,0:T(8,128)} %fusion.6, f32[4,128,1536]{2,1,0:T(8,128)} %fusion.8, bf16[1536,576,1]{1,0,2:T(8,128)(2,1)} %bitcast.171, bf16[4,128,576]{1,2,0:T(8,128)(2,1)} %param.23), kind=kOutput, calls=%fused_computation.5 | convolution fusion | flops 917766144 | bytes 13369344 | tf_op jit(solution)/shard_map/sbd,fd->sbf/dot_general | solution.py:438
  160.2 1.1 fusion.5
  161.8 1.4 multiply_reduce_fusion
  163.2 1.6 multiply_add_fusion
  164.9 1.4 convolution_convert_fusion
  166.3 2.1 copy.274.do_ref
  168.5 16.6 %shard_map.206 = (f32[4,128,576]{2,1,0:T(8,128)}, bf16[4,1024,384]{2,1,0:T(8,128)(2,1)}) custom-call(bf16[4,128,576]{2,1,0:T(8,128)(2,1)} %copy.264.q_ref, bf16[4,1024,384]{2,1,0:T(8,128)(2,1)} %shard_map.204.kv_ref, bf16[4,128,576]{2,1,0:T(8,128)(2,1)} %copy.274.do_ref, bf16[4,128,576]{2,1,0:T(8,128)(2,1)} %get-tuple-element.15.mixed_ref, ...), custom_call_target="tpu_custom_call" | custom-call | flops 9059696640 | bytes 6291456 | tf_op jit(solution)/shard_map/pallas_call | solution.py:215
  185.1 37.8 %shard_map.207 = bf16[8,4,128,384]{3,2,1,0:T(8,128)(2,1)} custom-call(bf16[4,1024,384]{2,1,0:T(8,128)(2,1)} %get-tuple-element.18.x_ref), custom_call_target="tpu_custom_call" | custom-call | tf_op jit(solution)/shard_map/pallas_call | solution.py:272
  222.9 2.4 convert_reduce_fusion
  227.0 1.6 bitcast_convert_fusion.4
  228.6 2.3 bitcast_convert_fusion.2
  230.9 2.4 bitcast_convert_fusion.1
  233.3 1.2 broadcast_multiply_fusion
  234.4 2.7 copy.275
  237.2 1.4 subtract_convert_fusion
  239.5 1.7 fusion.23
  241.2 1.2 copy.276
  243.1 1.1 copy.321
  244.2 1.1 fusion.12
  246.1 1.3 convolution_add_fusion
  247.4 1.2 fusion.19
  248.6 0.9 concatenate.62
  250.4 1.1 concatenate.54
  251.5 1.6 copy.280
  253.1 1.3 fusion.11
  255.8 2.0 copy.285
  257.8 2.3 concatenate.57
  260.1 3.6 concatenate.58
  263.7 3.6 concatenate.59
  267.5 11.2 %concatenate.61 = bf16[4,8,18,3649]{3,2,1,0:T(8,128)(2,1)} concatenate(bf16[4,8,18,576]{3,2,1,0:T(8,128)(2,1)} %concatenate.57, bf16[4,8,18,1536]{3,2,1,0:T(8,128)(2,1)} %concatenate.58, bf16[4,8,18,1536]{3,2,1,0:T(8,128)(2,1)} %concatenate.59, bf16[4,8,18,1]{3,2,1,0:T(8,128)(2,1)S(1)} %concatenate.63), dimensions={3} | concatenate | bytes 8407296 | tf_op jit(solution)/shard_map/concatenate | solution.py:463
  278.7 8.1 %copy.290 = bf16[4,8,18,3649]{3,0,2,1:T(4,128)(2,1)} copy(bf16[4,8,18,3649]{3,2,1,0:T(8,128)(2,1)} %concatenate.61) | data formatting | bytes 8407296 | tf_op jit(solution)/shard_map/concatenate | solution.py:463
  286.8 2.3 bitcast_convert_fusion
  289.1 3.9 copy.293
  294.3 116.8 %all-reduce.7.cloned.1.call-done = (bf16[4,8,18,961]{3,0,2,1:T(4,128)(2,1)}, bf16[4,8,18,3649]{3,0,2,1:T(4,128)(2,1)}, bf16[4,8,48,576]{3,2,1,0:T(8,128)(2,1)}) async-done(((bf16[4,8,18,961]{3,0,2,1:T(4,128)(2,1)}, bf16[4,8,18,3649]{3,0,2,1:T(4,128)(2,1)}, bf16[4,8,48,576]{3,2,1,0:T(8,128)(2,1)}), (bf16[4,8,18,961]{3,0,2,1:T(4,128)(2,1)}, bf16[4,8,18,3649]{3,0,2,1:T(4,128)(2,1)}, ...) | async-done | bytes 7080208
  411.1 1.9 dynamic-slice_bitcast_fusion
  414.0 1.6 dynamic-slice_bitcast_fusion.3
  416.4 2.3 dynamic-slice_bitcast_fusion.1
  418.8 18.4 %reduce-scatter.11.cloned.1.call-done = bf16[1,18,3649]{2,1,0:T(8,128)(2,1)} async-done(((bf16[4,18,3649]{2,1,0:T(8,128)(2,1)}), bf16[1,18,3649]{2,1,0:T(8,128)(2,1)}) %reduce-scatter.11.cloned.1.call-update) | async-done | bytes 131380
  437.2 1.8 copy.292
  439.1 1.2 fusion.18
  441.2 3.4 fusion.10
  444.6 13.4 %reduce-scatter.7.cloned.1.call-done = bf16[1,18,961]{2,1,0:T(8,128)(2,1)} async-done(((bf16[4,18,961]{2,1,0:T(8,128)(2,1)}), bf16[1,18,961]{2,1,0:T(8,128)(2,1)}) %reduce-scatter.7.cloned.1.call-update) | async-done | bytes 34612 | tf_op jit(solution)/shard_map/reduce_scatter | solution.py:347
  458.8 10.0 %all-gather.4 = bf16[1,144,961]{2,0,1:T(2,128)(2,1)S(1)} all-gather(bf16[1,18,961]{2,0,1:T(2,128)(2,1)S(1)} %copy.287), channel_id=6, replica_groups=mesh['ctx'=8,'fsdp'=4] {'ctx'}, dimensions={1}, use_global_device_ids=true | all-gather | bytes 311364 | tf_op jit(solution)/shard_map/all_gather | solution.py:348
  471.2 7.4 %reduce-scatter.9.cloned.1.call-done = bf16[1,48,576]{2,1,0:T(8,128)(2,1)} async-done(((bf16[4,48,576]{2,1,0:T(8,128)(2,1)}), bf16[1,48,576]{2,1,0:T(8,128)(2,1)}) %reduce-scatter.9.cloned.1.call-update) | async-done | bytes 55312 | tf_op jit(solution)/shard_map/reduce_scatter | solution.py:347
  478.6 10.1 %all-gather.6 = bf16[1,384,576]{2,1,0:T(8,128)(2,1)S(1)} all-gather(bf16[1,48,576]{2,1,0:T(8,128)(2,1)} %reduce-scatter.9.cloned.1.call-done), channel_id=8, replica_groups=mesh['ctx'=8,'fsdp'=4] {'ctx'}, dimensions={1}, use_global_device_ids=true | all-gather | bytes 497664 | tf_op jit(solution)/shard_map/all_gather | solution.py:348
  488.7 1.2 copy.294
  490.0 17.5 %all-gather.17.cloned.1.call-done = bf16[1,144,3649]{2,0,1:T(2,128)(2,1)} async-done(((bf16[1,18,3649]{2,0,1:T(2,128)(2,1)}), bf16[1,144,3649]{2,0,1:T(2,128)(2,1)}) %all-gather.17.cloned.1.call-update) | async-done | bytes 1050928 | tf_op jit(solution)/shard_map/all_gather | solution.py:348
  507.4 1.7 copy.328
  510.7 1.7 fusion.61
  (146 shorter events, 22.5 us)
Async XLA Ops:
  7.2 24.4 %copy-start = (bf16[384,576]{0,1:T(8,128)(2,1)S(1)}, bf16[384,576]{0,1:T(8,128)(2,1)}, u32[]{:S(2)}) copy-start(bf16[384,576]{0,1:T(8,128)(2,1)} %param.22) | copy-start | bytes 1327108
  7.2 135.3 %all-gather.13.cloned.1.call-start = ((), (), s32[]{:S(2)}) async-start(), calls=%async_computation.5 | async-start | bytes 4810752 | tf_op jit(solution)/shard_map/all_gather | solution.py:333
  30.4 16.0 %copy-start.24 = (bf16[144,576]{1,0:T(8,128)(2,1)S(1)}, bf16[144,576]{1,0:T(8,128)(2,1)}, u32[]{:S(2)}) copy-start(bf16[144,576]{1,0:T(8,128)(2,1)} %param.16) | copy-start | bytes 497668
  30.4 16.0 %copy-start.25 = (bf16[144,192]{1,0:T(8,128)(2,1)S(1)}, bf16[144,192]{1,0:T(8,128)(2,1)}, u32[]{:S(2)}) copy-start(bf16[144,192]{1,0:T(8,128)(2,1)} %param.18) | copy-start | bytes 165892
  30.4 16.0 %copy-start.26 = (bf16[144,192]{1,0:T(8,128)(2,1)S(1)}, bf16[144,192]{1,0:T(8,128)(2,1)}, u32[]{:S(2)}) copy-start(bf16[144,192]{1,0:T(8,128)(2,1)} %param.17) | copy-start | bytes 165892
  31.5 121.1 %all-gather.15.cloned.1.call-start = ((), (), s32[]{:S(2)}) async-start(), calls=%async_computation.6 | async-start | bytes 2211840 | tf_op jit(solution)/shard_map/all_gather | solution.py:333
  46.4 19.3 %copy-start.29 = (bf16[144]{0:T(256)(128)(2,1)S(1)}, bf16[144]{0:T(256)(128)(2,1)}, u32[]{:S(2)}) copy-start(bf16[144]{0:T(256)(128)(2,1)} %param.15) | copy-start | bytes 868
  46.4 19.4 %copy-start.30 = (bf16[144]{0:T(256)(128)(2,1)S(1)}, bf16[144]{0:T(256)(128)(2,1)}, u32[]{:S(2)}) copy-start(bf16[144]{0:T(256)(128)(2,1)} %param.14) | copy-start | bytes 868
  46.4 34.2 %copy-start.5 = (bf16[4,128,576]{1,2,0:T(8,128)(2,1)S(1)}, bf16[4,128,576]{1,2,0:T(8,128)(2,1)}, u32[]{:S(2)}) copy-start(bf16[4,128,576]{1,2,0:T(8,128)(2,1)} %param.12) | copy-start | bytes 1769476
  46.4 364.7 %all-reduce.7.cloned.1.call-start = ((), (), s32[]{:S(2)}) async-start(), calls=%async_computation.9 | async-start | bytes 14843904
  80.7 2.0 copy-start.4
  83.8 1.4 copy-start.27
  85.2 1.0 copy-start.20
  86.3 1.3 copy-start.23
  142.5 2.7 copy-start.16
  145.2 4.1 copy-start.2
  146.0 15.4 %copy-start.9 = (f32[4,128,576]{1,2,0:T(8,128)}, f32[4,128,576]{1,2,0:T(8,128)S(1)}, u32[]{:S(2)}) copy-start(f32[4,128,576]{1,2,0:T(8,128)S(1)} %get-tuple-element.125) | copy-start | bytes 3538948
  146.2 3.2 copy-start.6
  152.6 7.6 %copy-start.3 = (bf16[4,144,3648]{2,1,0:T(8,128)(2,1)S(1)}, bf16[4,144,3648]{2,1,0:T(8,128)(2,1)}, u32[]{:S(2)}) copy-start(bf16[4,144,3648]{2,1,0:T(8,128)(2,1)} %copy-done.2) | copy-start | bytes 12607492
  160.2 1.1 copy-start.35
  160.2 1.6 copy-start.32
  161.8 1.4 copy-start.18
  225.3 1.7 copy-start.17
  227.0 1.6 copy-start.7
  227.0 1.6 copy-start.36
  228.6 2.3 copy-start.33
  230.9 2.4 copy-start.13
  238.7 0.8 copy-start.11
  244.2 1.2 copy-start.21
  244.2 1.3 copy-start.8
  245.4 0.7 copy-start.14
  247.4 2.1 copy-start.22
  251.5 2.9 copy-start.12
  254.4 0.9 copy-start.15
  278.7 8.1 %copy-start.19 = (bf16[4,128,576]{1,2,0:T(8,128)(2,1)S(1)}, bf16[4,128,576]{1,2,0:T(8,128)(2,1)}, u32[]{:S(2)}) copy-start(bf16[4,128,576]{1,2,0:T(8,128)(2,1)} %param.23) | copy-start | bytes 1769476
  278.7 8.1 %copy-start.34 = (bf16[4,128,1536]{2,1,0:T(8,128)(2,1)S(1)}, bf16[4,128,1536]{2,1,0:T(8,128)(2,1)}, u32[]{:S(2)}) copy-start(bf16[4,128,1536]{2,1,0:T(8,128)(2,1)} %get-tuple-element.107) | copy-start | bytes 4718596
  293.0 0.7 copy-start.31
  293.1 144.1 %reduce-scatter.11.cloned.1.call-start = ((), (), s32[]{:S(2)}) async-start(), calls=%async_computation.8 | async-start | bytes 890880
  413.9 44.0 %reduce-scatter.7.cloned.1.call-start = ((), (), s32[]{:S(2)}) async-start(), calls=%async_computation.3 | async-start | bytes 245760 | tf_op jit(solution)/shard_map/reduce_scatter | solution.py:347
  416.4 62.2 %reduce-scatter.9.cloned.1.call-start = ((), (), s32[]{:S(2)}) async-start(), calls=%async_computation.4 | async-start | bytes 307200 | tf_op jit(solution)/shard_map/reduce_scatter | solution.py:347
  418.7 88.7 %all-gather.17.cloned.1.call-start = ((), (), s32[]{:S(2)}) async-start(), calls=%async_computation.7 | async-start | bytes 2405376 | tf_op jit(solution)/shard_map/all_gather | solution.py:348
  439.1 1.3 copy-start.10
  439.1 2.1 copy-start.28
  509.9 2.5 copy-start.1
Sparse Core Ops, SparseCore 0:
  31.6 36.9 all-gather.12
  70.5 47.8 all-gather.14
  293.2 117.8 all-reduce.6
  414.1 23.0 reduce-scatter.10
  439.9 18.0 reduce-scatter.6
  460.8 17.7 reduce-scatter.8
  481.1 26.3 all-gather.16

commit v2 on v1

--- a/solution.py
+++ b/solution.py
@@ -324,28 +324,67 @@
     return jnp.sum(parts.astype(jnp.float32), axis=0)
 
 
-def gather_shares(x):
-    count, rows = lax.axis_size("ctx"), x.shape[0]
-    if rows % count:
-        return lax.all_gather(x, "fsdp", axis=0, tiled=True)
-    share = lax.dynamic_slice_in_dim(x, lax.axis_index("ctx") * (rows // count), rows // count, 0)
-    along = lax.all_gather(share, "fsdp", axis=0, tiled=False)
-    whole = lax.all_gather(along, "ctx", axis=1, tiled=False)
-    return whole.reshape((-1,) + x.shape[1:])
-
-
-def reduce_rows(x):
-    count, parts = lax.axis_size("ctx"), lax.axis_size("fsdp")
-    rows = x.shape[0] // parts
-    x = x.astype(jnp.bfloat16)
-    if rows % count:
-        return lax.psum(
-            lax.psum_scatter(x, "fsdp", scatter_dimension=0, tiled=True), "ctx"
-        ).astype(jnp.float32)
-    x = x.reshape((parts, count, rows // count) + x.shape[1:])
-    x = lax.psum_scatter(x, "ctx", scatter_dimension=1, tiled=False)
-    x = lax.psum_scatter(x, "fsdp", scatter_dimension=0, tiled=False)
-    return lax.all_gather(x, "ctx", axis=0, tiled=True).astype(jnp.float32)
+def split_columns(matrix):
+    count = lax.axis_size("ctx")
+    return jnp.moveaxis(matrix.reshape(matrix.shape[0], count, -1), 1, 0)
+
+
+def join_columns(pieces):
+    return jnp.moveaxis(pieces, 0, 1).reshape(pieces.shape[1], -1)
+
+
+def split_down(matrix, parts, rows):
+    count = lax.axis_size("ctx")
+    down_rows = matrix.shape[0] // (parts * count)
+    groups = rows // down_rows
+    pieces = matrix.reshape(parts, count, down_rows, groups, -1)
+    return jnp.transpose(pieces, (1, 0, 3, 2, 4)).reshape(count, parts * rows, -1)
+
+
+def join_down(pieces, parts, down_rows):
+    count, rows, width = pieces.shape
+    groups = rows // parts // down_rows
+    split = pieces.reshape(count, parts, groups, down_rows, width)
+    return jnp.transpose(split, (1, 0, 3, 2, 4)).reshape(parts * count * down_rows, -1)
+
+
+def gather_shares(pieces):
+    share = lax.dynamic_index_in_dim(pieces, lax.axis_index("ctx"), 0, keepdims=False)
+    along = lax.all_gather(share, "fsdp", axis=0, tiled=True)
+    whole = lax.all_gather(along, "ctx", axis=0, tiled=True)
+    return whole.reshape((pieces.shape[0], -1) + pieces.shape[2:])
+
+
+def reduce_pieces(pieces):
+    count, rows, width = pieces.shape
+    mine = lax.psum_scatter(
+        pieces.reshape(count * rows, width), "ctx", scatter_dimension=0, tiled=True
+    )
+    mine = lax.psum_scatter(mine, "fsdp", scatter_dimension=0, tiled=True)
+    return lax.all_gather(mine, "ctx", axis=0, tiled=True).reshape(count, -1, width)
+
+
+def exchange_sum(pieces, axis, collective_id):
+    parts = exchange(
+        pieces,
+        axis,
+        pieces.shape[0],
+        lambda ref, peer: ref.at[peer],
+        lambda ref, me: ref.at[me],
+        pieces.shape,
+        collective_id,
+    )
+    return jnp.sum(parts.astype(jnp.float32), axis=0)
+
+
+def reduce_pieces_now(pieces, first_id):
+    count, rows, width = pieces.shape
+    mine = exchange_sum(pieces, "ctx", first_id).astype(jnp.bfloat16)
+    parts = lax.axis_size("fsdp")
+    mine = exchange_sum(mine.reshape(parts, rows // parts, width), "fsdp", first_id + 1)
+    return gather_rows(mine.astype(jnp.bfloat16), "ctx", first_id + 2).reshape(
+        count, rows // parts, width
+    )
 
 def body(
     tokens,
@@ -365,24 +404,46 @@
     half_size = rows_per_block // 2
     score_scale = HEAD_DIMENSION ** (-0.5)
     ctx_index = lax.axis_index("ctx")
-    first_pack = gather_rows(
-        jnp.concatenate([query_weight, key_matrix, value_matrix], axis=1), "fsdp", 0
-    )
+    count = lax.axis_size("ctx")
+    parts = lax.axis_size("fsdp")
+    rows_owned = query_weight.shape[0]
     kv_width = KEY_VALUE_HEADS * HEAD_DIMENSION
     query_width = query_weight.shape[1]
     ff_width = gate_weight.shape[1]
-    gains = lax.all_gather(jnp.stack([gain_one, gain_two]), "fsdp", axis=1, tiled=True)
-    second_pack = gather_shares(jnp.concatenate([out_weight, gate_weight, up_weight], axis=1))
+    down_rows = down_weight.shape[0] // count
+    down_end = ff_width // count
+    gate_end = down_end + ff_width // count
+    up_end = gate_end + ff_width // count
+    filler = jnp.zeros((rows_owned, -(query_width + 2 * kv_width + 2) % 128), gain_one.dtype)
+    first_pack = gather_rows(
+        jnp.concatenate(
+            [query_weight, key_matrix, value_matrix, gain_one[:, None], gain_two[:, None], filler],
+            axis=1,
+        ),
+        "fsdp",
+        0,
+    )
+    second_pack = gather_shares(
+        jnp.concatenate(
+            [
+                split_down(down_weight, 1, rows_owned),
+                split_columns(gate_weight),
+                split_columns(up_weight),
+                split_columns(out_weight),
+            ],
+            axis=2,
+        )
+    )
     gathered = (
-        gains[0],
-        gains[1],
+        first_pack[:, query_width + 2 * kv_width],
+        first_pack[:, query_width + 2 * kv_width + 1],
         first_pack[:, :query_width],
         first_pack[:, query_width : query_width + kv_width],
-        first_pack[:, query_width + kv_width :],
-        second_pack[:, :model_width],
-        second_pack[:, model_width : model_width + ff_width],
-        second_pack[:, model_width + ff_width :],
-        gather_shares(down_weight),
+        first_pack[:, query_width + kv_width : query_width + 2 * kv_width],
+        join_columns(second_pack[:, :, up_end:]),
+        join_columns(second_pack[:, :, down_end:gate_end]),
+        join_columns(second_pack[:, :, gate_end:up_end]),
+        join_down(second_pack[:, :, :down_end], parts, down_rows),
     )
     gain_first = gathered[0].astype(jnp.float32)
     gain_second = gathered[1].astype(jnp.float32)
@@ -458,10 +519,18 @@
     mixed_gradient = jnp.einsum(
         "sbd,qd->sbq", grad_branch, out_full, preferred_element_type=jnp.float32
     ).astype(jnp.bfloat16)
-    owned_down = reduce_rows(down_grad)
-    owned_early = reduce_rows(
-        jnp.concatenate([out_grad, gate_grad, up_grad, gain_two_grad[:, None]], axis=1)
-    )
+    bf16 = jnp.bfloat16
+    early = reduce_pieces(
+        jnp.concatenate(
+            [
+                split_down(down_grad.astype(bf16), parts, rows_owned),
+                split_columns(gate_grad.astype(bf16)),
+                split_columns(up_grad.astype(bf16)),
+                split_columns(out_grad.astype(bf16)),
+            ],
+            axis=2,
+        )
+    ).astype(jnp.float32)
     query_sum, key_value_part = attend_back(
         scaled_query,
         key_value,
@@ -510,19 +579,27 @@
     grad_tokens = (grad_middle + norm_back(grad_normed, base_one, gain_first, scale_one)).astype(
         jnp.bfloat16
     )
-    owned_late = reduce_rows(
-        jnp.concatenate([query_grad, key_grad, value_grad, gain_one_grad[:, None]], axis=1)
-    )
+    gain_grads = jnp.stack([gain_one_grad, gain_two_grad], axis=1).astype(bf16)
+    columns = [split_columns(g.astype(bf16)) for g in (query_grad, key_grad, value_grad)]
+    gain_columns = jnp.broadcast_to(gain_grads[None], (count,) + gain_grads.shape)
+    used = sum(g.shape[2] for g in columns) + 2
+    filler = jnp.zeros((count, model_width, -used % 128), bf16)
+    late = reduce_pieces_now(
+        jnp.concatenate(columns + [gain_columns, filler], axis=2), 3
+    ).astype(jnp.float32)
+    query_end = query_width // count
+    key_end = query_end + kv_width // count
+    value_end = key_end + kv_width // count
     owned = (
-        owned_late[:, -1],
-        owned_early[:, -1],
-        owned_late[:, :query_width],
-        owned_late[:, query_width : query_width + kv_width],
-        owned_late[:, query_width + kv_width : query_width + 2 * kv_width],
-        owned_early[:, :model_width],
-        owned_early[:, model_width : model_width + ff_width],
-        owned_early[:, model_width + ff_width : model_width + 2 * ff_width],
-        owned_down,
+        late[0, :, value_end],
+        late[0, :, value_end + 1],
+        join_columns(late[:, :, :query_end]),
+        join_columns(late[:, :, query_end:key_end]),
+        join_columns(late[:, :, key_end:value_end]),
+        join_columns(early[:, :, up_end:]),
+        join_columns(early[:, :, down_end:gate_end]),
+        join_columns(early[:, :, gate_end:up_end]),
+        join_down(early[:, :, :down_end], 1, down_rows),
     )
     return (output, grad_tokens) + tuple(owned)
 

time: 527 us -> 449 us (0.85)
  waiting for transfers between devices: 174 us -> 24.5 us
  Pallas kernels: 125 us -> 188 us
  blocking collectives: 69.8 us -> 23.1 us
  local copies, waits for them, and re-layouts: 79.9 us -> 115 us
  other arithmetic: 14.5 us -> 29.4 us
    unnamed x9 -> x4, waiting for transfers between devices: 135 us -> 0.07 us
    pallas_call x3 -> x6, Pallas kernels: 95.7 us -> 159 us  [exchange(): pl.pallas_call(functools.partial(exchange_kernel, axis, count, source, ta...]
    all_gather x5 -> x1, blocking collectives: 69.8 us -> 23.1 us  [gather_shares(): along = lax.all_gather(share, 'fsdp', axis=0, tiled=True)]
    reshape x0 -> x14, local copies, waits for them, and re-layouts: none -> 29.8 us  [the longest x7 9.4 us: split_columns(): return jnp.moveaxis(matrix.reshape(matrix.shape[0], count, -1), 1, 0)]
    transpose x0 -> x15, local copies, waits for them, and re-layouts: none -> 22.8 us  [the longest x11 16.7 us: join_columns(): return jnp.moveaxis(pieces, 0, 1).reshape(pieces.shape[1], -1)]
    concatenate x10 -> x5, local copies, waits for them, and re-layouts: 35.6 us -> 18 us  [the longest x3 10.2 us: body(): jnp.concatenate([split_down(down_grad.astype(bf16), parts, rows_owned), s...]
    all_gather x3 -> x2, waiting for transfers between devices: 17.5 us -> 0.01 us  [the longest x1 0.01 us: gather_shares(): whole = lax.all_gather(along, 'ctx', axis=0, tiled=True)]
    reduce_scatter x7 -> x0, local copies, waits for them, and re-layouts: 10.1 us -> none  [the longest x5 7.45 us: reduce_rows(): x = lax.psum_scatter(x, 'ctx', scatter_dimension=1, tiled=False)]
  transfers between devices with their start and end apart: 7 -> 4, of which waited for: 5 -> 2; matrix products, arithmetic and copies ran while one was open for 7% -> 16% of each run, Pallas kernels for 14% -> 43%
where the time goes in v2:
time: 449 us; the launch traced here: 441 us
  Pallas kernels  188 us (42%)
  local copies, waits for them, and re-layouts  115 us (26%)
  matrix products  46 us (10%)
  other arithmetic  29.4 us (7%)
  waiting for transfers between devices  24.5 us (5%)
  blocking collectives  23.1 us (5%)
  between operations  14.7 us (3%)
    pallas_call x6, Pallas kernels, exchange(): pl.pallas_call(functools.partial(exchange_kernel, axis, count, source, ta...  159 us
    all_gather x1, blocking collectives, gather_shares(): along = lax.all_gather(share, 'fsdp', axis=0, tiled=True)  23.1 us
    transpose x11, local copies, waits for them, and re-layouts, join_columns(): return jnp.moveaxis(pieces, 0, 1).reshape(pieces.shape[1], -1)  16.7 us
    pallas_call x1, Pallas kernels, attend_back(): pl.pallas_call(backward_kernel, grid=(seqs,), in_specs=[seq_spec(rows, wi...  16.5 us
    unnamed x90, local copies, waits for them, and re-layouts  12.8 us
    pallas_call x1, Pallas kernels, attend(): pl.pallas_call(forward_kernel, grid=(seqs,), in_specs=[seq_spec(rows, wid...  12.5 us
    reduce_scatter x1, waiting for transfers between devices, reduce_pieces(): mine = lax.psum_scatter(mine, 'fsdp', scatter_dimension=0, tiled=True)  12.4 us
    reduce_scatter x1, waiting for transfers between devices, reduce_pieces(): lax.psum_scatter(pieces.reshape(count * rows, width), 'ctx', scatter_dime...  12 us
  transfers between devices with their start and end apart: 4, of which 2 were waited for; matrix products, arithmetic and copies ran while one was open for 16% of the time, Pallas kernels for 43%

profile of v2, /device:TPU:0, one launch (start us, length us, event | category | flops | bytes accessed | tf_op | source)
XLA Modules:
  0.0 441.4 jit_solution(2467921822405475292)
XLA Ops:
  10.7 23.1 %all-gather = bf16[1,576,648]{2,1,0:T(8,128)(2,1)} all-gather(bf16[1,144,648]{2,1,0:T(8,128)(2,1)S(1)} %fusion.47), channel_id=2, replica_groups=mesh['ctx'=8,'fsdp'=4] {'fsdp'}, dimensions={1}, use_global_device_ids=true | all-gather | bytes 933120 | tf_op jit(solution)/shard_map/all_gather | solution.py:353
  35.0 20.8 %shard_map.203 = bf16[576,1024]{1,0:T(8,128)(2,1)} custom-call(bf16[144,1024]{1,0:T(8,128)(2,1)} %concatenate.45.x_ref), custom_call_target="tpu_custom_call" | custom-call | tf_op jit(solution)/shard_map/pallas_call | solution.py:272
  55.9 1.9 convert_reduce_fusion.1
  58.7 2.1 fusion.26
  64.6 47.3 %shard_map.204.kv_ref = bf16[4,1024,384]{2,1,0:T(8,128)(2,1)} custom-call(bf16[4,128,384]{2,1,0:T(8,128)(2,1)} %pad_maximum_fusion.2.x_ref), custom_call_target="tpu_custom_call" | custom-call | tf_op jit(solution)/shard_map/pallas_call | solution.py:272
  113.7 12.5 %shard_map.205 = (bf16[4,128,576]{2,1,0:T(8,128)(2,1)}, f32[4,16,128]{2,1,0:T(8,128)}) custom-call(bf16[4,128,576]{2,1,0:T(8,128)(2,1)} %copy.362.q_ref, bf16[4,1024,384]{2,1,0:T(8,128)(2,1)} %shard_map.204.kv_ref, s32[1,128]{1,0:T(1,128)} %fusion.55.qpos_ref, s32[1024,1]{1,0:T(8,128)} %fusion.30.kpos_ref), custom_call_target="tpu_custom_call" | custom-call | flops 3623878656 | bytes 3145728 | tf_op jit(solution)/shard_map/pallas_call | solution.py:195
  126.2 2.1 slice_bitcast_fusion.4
  128.3 7.1 %fusion.64 = (bf16[8,576,192]{2,1,0:T(8,128)(2,1)}, bf16[576,8,192]{2,0,1:T(8,128)(2,1)S(1)}, bf16[576,8,192]{2,0,1:T(8,128)(2,1)}) fusion(bf16[8,576,648]{2,1,0:T(8,128)(2,1)} %bitcast.177), kind=kLoop, calls=%fused_computation.139 | loop fusion | bytes 10616832 | tf_op jit(solution)/shard_map/slice | solution.py:446
  136.8 2.1 multiply_reduce_fusion.2
  139.5 4.3 copy.371
  143.8 2.4 copy.373
  147.1 5.0 %fusion.67 = f32[4,128,1536]{2,1,0:T(8,128)} fusion(bf16[4,128,576]{1,2,0:T(8,128)(2,1)S(1)} %multiply_convert_fusion.3, bf16[576,1536,1]{0,1,2:T(8,128)(2,1)} %bitcast.202), kind=kOutput, calls=%fused_computation.142 | convolution fusion | flops 905969664 | bytes 5505024 | tf_op jit(solution)/shard_map/dot_general | solution.py:490
  152.1 3.1 fusion.68
  155.2 3.2 copy.376
  158.5 7.3 %reshape.432 = bf16[1536,576]{1,0:T(8,128)(2,1)} reshape(bf16[4,8,48,3,192]{4,3,2,1,0:T(4,128)(2,1)} %copy.376) | data formatting | bytes 3538944 | tf_op jit(solution)/shard_map/reshape | solution.py:348
  165.8 7.6 %multiply_convert_fusion = (bf16[4,128,1536]{2,1,0:T(8,128)(2,1)S(1)}, bf16[4,128,1536]{2,1,0:T(8,128)(2,1)S(1)}, bf16[4,128,1536]{2,1,0:T(8,128)(2,1)}) fusion(f32[4,128,1536]{2,1,0:T(8,128)} %fusion.67, f32[4,128,1536]{2,1,0:T(8,128)} %fusion.68, bf16[4,128,576]{1,2,0:T(8,128)(2,1)} %param.23, bf16[1536,576]{1,0:T(8,128)(2,1)} %reshape.432), kind=kOutput, calls=%fused_computation.6 | convolution fusion | flops 917766144 | bytes 13369344 | tf_op jit(solution)/shard_map/sbd,fd->sbf/dot_general | solution.py:499
  174.5 2.3 bitcast_convert_fusion.1
  176.8 2.3 bitcast_convert_fusion
  179.2 2.0 multiply_reduce_fusion
  182.2 1.5 bitcast_convert_fusion.3
  183.7 1.6 copy.447
  185.3 3.9 copy.403
  189.2 4.3 copy.446
  193.5 3.9 copy.401
  197.4 4.3 copy.445
  201.6 3.9 bitcast_convert_fusion.2
  205.5 3.9 copy.399
  209.4 7.3 %reshape.442 = bf16[4,8,48,3,192]{4,3,2,1,0:T(4,128)(2,1)} reshape(bf16[1536,576]{1,0:T(8,128)(2,1)} %copy.399) | data formatting | bytes 3538944 | tf_op jit(solution)/shard_map/reshape | solution.py:340
  216.7 2.5 copy.400
  220.0 5.8 %pad_maximum_fusion = bf16[4608,648]{1,0:T(8,128)(2,1)} fusion(bf16[4608,72]{1,0:T(8,128)(2,1)S(1)} %bitcast.195, bf16[4608,192]{1,0:T(8,128)(2,1)S(1)} %bitcast.179, bf16[4608,192]{1,0:T(8,128)(2,1)S(1)} %bitcast.180, bf16[4608,192]{1,0:T(8,128)(2,1)S(1)} %bitcast.181), kind=kLoop, calls=%fused_computation | loop fusion | flops 23887872 | bytes 11943936 | tf_op jit(solution)/shard_map/concatenate | solution.py:524
  226.9 1.5 convolution_convert_fusion
  228.4 2.1 copy.384.do_ref
  230.5 16.5 %shard_map.206 = (f32[4,128,576]{2,1,0:T(8,128)}, bf16[4,1024,384]{2,1,0:T(8,128)(2,1)}) custom-call(bf16[4,128,576]{2,1,0:T(8,128)(2,1)} %copy.362.q_ref, bf16[4,1024,384]{2,1,0:T(8,128)(2,1)} %shard_map.204.kv_ref, bf16[4,128,576]{2,1,0:T(8,128)(2,1)} %copy.384.do_ref, bf16[4,128,576]{2,1,0:T(8,128)(2,1)} %get-tuple-element.15.mixed_ref, ...), custom_call_target="tpu_custom_call" | custom-call | flops 9059696640 | bytes 6291456 | tf_op jit(solution)/shard_map/pallas_call | solution.py:215
  247.0 57.3 %shard_map.207 = bf16[8,4,128,384]{3,2,1,0:T(8,128)(2,1)} custom-call(bf16[4,1024,384]{2,1,0:T(8,128)(2,1)} %get-tuple-element.18.x_ref), custom_call_target="tpu_custom_call" | custom-call | tf_op jit(solution)/shard_map/pallas_call | solution.py:272
  304.3 2.4 convert_reduce_fusion
  309.2 2.8 copy.385
  313.1 12.0 %reduce-scatter.3.cloned.1.call-done = bf16[576,648]{1,0:T(8,128)(2,1)} async-done(((bf16[4608,648]{1,0:T(8,128)(2,1)}), bf16[576,648]{1,0:T(8,128)(2,1)}) %reduce-scatter.3.cloned.1.call-update) | async-done | bytes 746512 | tf_op jit(solution)/shard_map/reduce_scatter | solution.py:360
  325.3 1.5 subtract_convert_fusion
  326.8 1.6 bitcast_convert_fusion.4
  328.5 2.4 copy.390
  332.0 1.9 fusion.14
  333.9 2.4 copy.391
  337.4 2.4 copy.392
  339.8 12.4 %reduce-scatter.5.cloned.1.call-done = bf16[144,648]{1,0:T(8,128)(2,1)} async-done(((bf16[576,648]{1,0:T(8,128)(2,1)}), bf16[144,648]{1,0:T(8,128)(2,1)}) %reduce-scatter.5.cloned.1.call-update) | async-done | bytes 186640 | tf_op jit(solution)/shard_map/reduce_scatter | solution.py:363
  352.2 2.0 fusion.24
  354.6 1.5 fusion.22
  358.7 7.0 %concatenate.52.x_ref = bf16[8,576,128]{2,1,0:T(8,128)(2,1)} concatenate(bf16[8,576,72]{2,1,0:T(8,128)(2,1)} %bitcast.190, bf16[8,576,24]{2,1,0:T(8,128)(2,1)} %bitcast.191, bf16[8,576,24]{2,1,0:T(8,128)(2,1)} %bitcast.192, bf16[8,576,2]{2,1,0:T(8,128)(2,1)} %broadcast_in_dim.41, bf16[8,576,6]{2,1,0:T(8,128)(2,1)} %broadcast_in_dim.68), dimensions={2} | concatenate | bytes 2359296 | tf_op jit(solution)/shard_map/concatenate | solution.py:588
  365.7 20.7 %shard_map.208 = bf16[8,576,128]{2,1,0:T(8,128)(2,1)} custom-call(bf16[8,576,128]{2,1,0:T(8,128)(2,1)} %concatenate.52.x_ref), custom_call_target="tpu_custom_call" | custom-call | tf_op jit(solution)/shard_map/pallas_call | solution.py:272
  386.5 2.1 reduce_sum.114
  388.6 6.6 %shard_map.209 = bf16[4,144,128]{2,1,0:T(8,128)(2,1)} custom-call(bf16[4,144,128]{2,1,0:T(8,128)(2,1)} %bitcast.213), custom_call_target="tpu_custom_call" | custom-call | tf_op jit(solution)/shard_map/pallas_call | solution.py:272
  395.2 1.6 reduce_sum.115.x_ref
  396.8 6.4 %shard_map.210 = bf16[1152,128]{1,0:T(8,128)(2,1)} custom-call(bf16[144,128]{1,0:T(8,128)(2,1)} %reduce_sum.115.x_ref), custom_call_target="tpu_custom_call" | custom-call | tf_op jit(solution)/shard_map/pallas_call | solution.py:272
  403.2 1.8 convert.52
  409.3 2.0 reshape.439
  412.6 1.4 copy.459
  414.7 1.4 copy.460
  416.9 2.6 fusion.21
  419.4 1.9 fusion.11
  421.4 1.8 convert.53
  423.4 1.4 slice_bitcast_fusion.2
  426.4 2.0 copy.411
  428.4 1.3 reshape.447
  431.7 1.4 copy.448
  433.1 1.6 reshape.479
  (163 shorter events, 37.8 us)
Async XLA Ops:
  7.2 1.4 copy-start.20
  7.2 1.9 copy-start.21
  7.2 119.0 %all-gather.7.cloned.1.call-start = ((), (), s32[]{:S(2)}) async-start(), calls=%async_computation.5 | async-start | bytes 7962624 | tf_op jit(solution)/shard_map/all_gather | solution.py:354
  8.6 1.0 copy-start.19
  10.6 23.2 %copy-start.36 = (bf16[144]{0:T(256)(128)(2,1)S(1)}, bf16[144]{0:T(256)(128)(2,1)}, u32[]{:S(2)}) copy-start(bf16[144]{0:T(256)(128)(2,1)} %param.14) | copy-start | bytes 868
  10.7 23.3 %copy-start.37 = (bf16[144]{0:T(256)(128)(2,1)S(1)}, bf16[144]{0:T(256)(128)(2,1)}, u32[]{:S(2)}) copy-start(bf16[144]{0:T(256)(128)(2,1)} %param.15) | copy-start | bytes 868
  10.7 23.4 %copy-start.22 = (bf16[144,576]{1,0:T(8,128)(2,1)S(1)}, bf16[144,576]{1,0:T(8,128)(2,1)}, u32[]{:S(2)}) copy-start(bf16[144,576]{1,0:T(8,128)(2,1)} %param.16) | copy-start | bytes 497668
  10.7 23.4 %copy-start.25 = (bf16[144,192]{1,0:T(8,128)(2,1)S(1)}, bf16[144,192]{1,0:T(8,128)(2,1)}, u32[]{:S(2)}) copy-start(bf16[144,192]{1,0:T(8,128)(2,1)} %param.17) | copy-start | bytes 165892
  10.7 23.4 %copy-start.26 = (bf16[144,192]{1,0:T(8,128)(2,1)S(1)}, bf16[144,192]{1,0:T(8,128)(2,1)}, u32[]{:S(2)}) copy-start(bf16[144,192]{1,0:T(8,128)(2,1)} %param.18) | copy-start | bytes 165892
  33.8 22.0 %copy-start.38 = (s32[16]{0:T(128)S(1)}, s32[16]{0:T(128)}, u32[]{:S(2)}) copy-start(s32[16]{0:T(128)} %param.13) | copy-start | bytes 196
  33.8 291.3 %reduce-scatter.3.cloned.1.call-start = ((), (), s32[]{:S(2)}) async-start(), calls=%async_computation.2 | async-start | bytes 7962624 | tf_op jit(solution)/shard_map/reduce_scatter | solution.py:360
  34.1 23.7 %copy-start.2 = (bf16[4,128,576]{1,2,0:T(8,128)(2,1)S(1)}, bf16[4,128,576]{1,2,0:T(8,128)(2,1)}, u32[]{:S(2)}) copy-start(bf16[4,128,576]{1,2,0:T(8,128)(2,1)} %param.12) | copy-start | bytes 1769476
  57.8 5.1 %copy-start.28 = (f32[576]{0:T(1024)}, f32[576]{0:T(1024)S(1)}, u32[]{:S(2)}) copy-start(f32[576]{0:T(1024)S(1)} %get-tuple-element.90) | copy-start | bytes 6916
  58.0 4.9 %copy-start.32 = (f32[4,128]{1,0:T(4,128)}, f32[4,128]{1,0:T(4,128)S(1)}, u32[]{:S(2)}) copy-start(f32[4,128]{1,0:T(4,128)S(1)} %add_rsqrt_fusion.1) | copy-start | bytes 6148
  61.0 1.3 copy-start.7
  147.1 5.1 %copy-start.17 = (bf16[4,128,576]{1,2,0:T(8,128)(2,1)}, bf16[4,128,576]{1,2,0:T(8,128)(2,1)S(1)}, u32[]{:S(2)}) copy-start(bf16[4,128,576]{1,2,0:T(8,128)(2,1)S(1)} %multiply_convert_fusion.3) | copy-start | bytes 1769476
  147.1 5.0 %copy-start.6 = (bf16[576,8,192]{0,2,1:T(8,128)(2,1)S(1)}, bf16[576,8,192]{0,2,1:T(8,128)(2,1)}, u32[]{:S(2)}) copy-start(bf16[576,8,192]{0,2,1:T(8,128)(2,1)} %copy.373) | copy-start | bytes 5308420
  152.1 3.1 copy-start.1
  165.8 7.6 %copy-start.14 = (bf16[576,8,192]{0,2,1:T(8,128)(2,1)S(1)}, bf16[576,8,192]{0,2,1:T(8,128)(2,1)}, u32[]{:S(2)}) copy-start(bf16[576,8,192]{0,2,1:T(8,128)(2,1)} %copy.371) | copy-start | bytes 5308420
  173.3 1.1 copy-start.18
  176.8 2.3 copy-start.27
  176.8 2.3 copy-start.31
  179.2 2.0 copy-start.16
  181.1 1.1 copy-start.11
  216.7 2.6 copy-start.4
  216.7 3.3 copy-start.5
  225.8 1.1 copy-start.9
  225.8 126.4 %reduce-scatter.5.cloned.1.call-start = ((), (), s32[]{:S(2)}) async-start(), calls=%async_computation.3 | async-start | bytes 1105920 | tf_op jit(solution)/shard_map/reduce_scatter | solution.py:363
  306.7 1.4 copy-start.15
  312.0 13.2 %copy-start.23 = (f32[128,32]{0,1:T(8,128)S(1)}, f32[128,32]{0,1:T(8,128)}, u32[]{:S(2)}) copy-start(f32[128,32]{0,1:T(8,128)} %get-tuple-element.111) | copy-start | bytes 49156
  325.2 96.2 %all-gather.5.cloned.1.call-start = ((), (), s32[]{:S(2)}) async-start(), calls=%async_computation.4 | async-start | bytes 1990656 | tf_op jit(solution)/shard_map/all_gather | solution.py:364
  325.2 1.6 copy-start.3
  325.2 1.6 copy-start.29
  325.2 1.6 copy-start.33
  326.8 1.7 copy-start.12
  328.5 2.4 copy-start.24
  332.0 4.3 copy-start.30
  332.0 4.3 copy-start.34
  336.3 3.5 copy-start.35
  352.2 2.0 copy-start.8
  408.3 3.0 copy-start
  416.8 2.6 copy-start.13
  416.8 2.6 copy-start.39
  423.4 1.8 copy-start.10
Sparse Core Ops, SparseCore 0:
  33.9 76.2 all-gather.6
  225.9 99.1 reduce-scatter.2
  327.6 24.5 reduce-scatter.4
  354.1 33.1 all-gather.4
